TPU v7x, 32 devices: a whole 2x2x4 slice. The times are simulated.
32 devices in a mesh: dp: 8 (over y, x, core), blk: 4 (over z).
Axes of the slice: x: 2, y: 2, z: 4, core: 2. Of those that a mesh axis runs over, the one named last changes fastest.
Arguments:
- tokens: bfloat16 [24, 1536, 768], P('dp', 'blk'), may hold values from -6 to 6
- counts: int32 [24], P('dp'), may hold values from 864 to 1536, as said below
- ln1_gain: bfloat16 [768], replicated, may hold values from 0.5 to 1.5
- ln1_shift: bfloat16 [768], replicated, may hold values from -0.59765625 to 0.59765625
- w_qkv: bfloat16 [768, 2304], replicated, may hold values from -0.21875 to 0.21875
- bias_q: bfloat16 [768], replicated, may hold values from -0.59765625 to 0.59765625
- bias_v: bfloat16 [768], replicated, may hold values from -0.23925781 to 0.23925781
- w_out: bfloat16 [768, 768], replicated, may hold values from -4 to 4
- bias_out: bfloat16 [768], replicated, may hold values from -0.59765625 to 0.59765625
- ln2_gain: bfloat16 [768], replicated, may hold values from 0.5 to 1.5
- ln2_shift: bfloat16 [768], replicated, may hold values from -0.59765625 to 0.59765625
- w_fc1: bfloat16 [768, 3072], replicated, may hold values from -0.21875 to 0.21875
- bias_fc1: bfloat16 [3072], replicated, may hold values from -0.59765625 to 0.59765625
- w_fc2: bfloat16 [3072, 768], replicated, may hold values from -0.109375 to 0.109375
- bias_fc2: bfloat16 [768], replicated, may hold values from -0.59765625 to 0.59765625
- cotangent: bfloat16 [24, 1536, 768], P('dp', 'blk'), may hold values from -6 to 6
Outputs:
- output: bfloat16 [24, 1536, 768], P('dp', 'blk')
- input_grad: float32 [24, 1536, 768], P('dp', 'blk')
- grad_ln1_gain: float32 [768], replicated
- grad_ln1_shift: float32 [768], replicated
- grad_w_qkv: float32 [768, 2304], replicated
- grad_bias_q: float32 [768], replicated
- grad_bias_v: float32 [768], replicated
- grad_w_out: float32 [768, 768], replicated
- grad_bias_out: float32 [768], replicated
- grad_ln2_gain: float32 [768], replicated
- grad_ln2_shift: float32 [768], replicated
- grad_w_fc1: float32 [768, 3072], replicated
- grad_bias_fc1: float32 [3072], replicated
- grad_w_fc2: float32 [3072, 768], replicated
- grad_bias_fc2: float32 [768], replicated
Inputs may be any that keep to these rules, and one draw needn't show every extreme that they name: `counts`: each cube holds its valid tokens first; in each index of dp exactly the ceiling of half of its 3 cubes hold 1536, the others 864.
All inputs are finite; a program needn't handle non-finite values.
Results may differ from a plain program's by a relative error of at most 0.02.
Values may be sent and summed in bfloat16 or wider, within the bound.
No kernel may reach another device: no remote copies, remote signals or barrier semaphores. Data moves between devices by JAX's collectives and lax.ppermute only.
A program may use at most 256 MiB of HBM per device.

v0:
```python
import math

import jax
import jax.numpy as jnp
from jax import lax
from jax.sharding import PartitionSpec as P

HEADS = 12
HD = 64


NORM_EPS = 1e-06
MASK_LOW = -1e30


def norm_rows(values, gain, shift):
    centre = values - jnp.mean(values, axis=-1, keepdims=True)
    spread = jnp.mean(centre * centre, axis=-1, keepdims=True)
    return centre * lax.rsqrt(spread + NORM_EPS) * gain + shift


def gelu_exact(values):
    return jax.nn.gelu(values, approximate=False)


def cube_valid(counts, offset, length):
    places = offset + jnp.arange(length, dtype=jnp.int32)
    return places[None, :] < counts[:, None]


def total_every(parts):
    split = (
        lax.psum_scatter(
            parts[0].astype(jnp.bfloat16), "blk", scatter_dimension=0, tiled=True
        ).astype(jnp.float32),
        lax.psum_scatter(
            parts[1].astype(jnp.bfloat16), "blk", scatter_dimension=0, tiled=True
        ).astype(jnp.float32),
        lax.psum_scatter(
            parts[2].astype(jnp.bfloat16), "blk", scatter_dimension=0, tiled=True
        ).astype(jnp.float32),
        lax.psum_scatter(
            parts[3].astype(jnp.bfloat16), "blk", scatter_dimension=0, tiled=True
        ).astype(jnp.float32),
        lax.psum_scatter(
            parts[4].astype(jnp.bfloat16), "blk", scatter_dimension=0, tiled=True
        ).astype(jnp.float32),
        lax.psum_scatter(
            parts[5].astype(jnp.bfloat16), "blk", scatter_dimension=0, tiled=True
        ).astype(jnp.float32),
        lax.psum_scatter(
            parts[6].astype(jnp.bfloat16), "blk", scatter_dimension=0, tiled=True
        ).astype(jnp.float32),
        lax.psum_scatter(
            parts[7].astype(jnp.bfloat16), "blk", scatter_dimension=0, tiled=True
        ).astype(jnp.float32),
        lax.psum_scatter(
            parts[8].astype(jnp.bfloat16), "blk", scatter_dimension=0, tiled=True
        ).astype(jnp.float32),
        lax.psum_scatter(
            parts[9].astype(jnp.bfloat16), "blk", scatter_dimension=0, tiled=True
        ).astype(jnp.float32),
        lax.psum_scatter(
            parts[10].astype(jnp.bfloat16), "blk", scatter_dimension=0, tiled=True
        ).astype(jnp.float32),
        lax.psum_scatter(
            parts[11].astype(jnp.bfloat16), "blk", scatter_dimension=0, tiled=True
        ).astype(jnp.float32),
        lax.psum_scatter(
            parts[12].astype(jnp.bfloat16), "blk", scatter_dimension=0, tiled=True
        ).astype(jnp.float32),
    )
    summed = (
        lax.psum(split[0].astype(jnp.bfloat16), "dp").astype(jnp.float32),
        lax.psum(split[1].astype(jnp.bfloat16), "dp").astype(jnp.float32),
        lax.psum(split[2].astype(jnp.bfloat16), "dp").astype(jnp.float32),
        lax.psum(split[3].astype(jnp.bfloat16), "dp").astype(jnp.float32),
        lax.psum(split[4].astype(jnp.bfloat16), "dp").astype(jnp.float32),
        lax.psum(split[5].astype(jnp.bfloat16), "dp").astype(jnp.float32),
        lax.psum(split[6].astype(jnp.bfloat16), "dp").astype(jnp.float32),
        lax.psum(split[7].astype(jnp.bfloat16), "dp").astype(jnp.float32),
        lax.psum(split[8].astype(jnp.bfloat16), "dp").astype(jnp.float32),
        lax.psum(split[9].astype(jnp.bfloat16), "dp").astype(jnp.float32),
        lax.psum(split[10].astype(jnp.bfloat16), "dp").astype(jnp.float32),
        lax.psum(split[11].astype(jnp.bfloat16), "dp").astype(jnp.float32),
        lax.psum(split[12].astype(jnp.bfloat16), "dp").astype(jnp.float32),
    )
    return (
        lax.all_gather(summed[0].astype(jnp.bfloat16), "blk", axis=0, tiled=True).astype(
            jnp.float32
        ),
        lax.all_gather(summed[1].astype(jnp.bfloat16), "blk", axis=0, tiled=True).astype(
            jnp.float32
        ),
        lax.all_gather(summed[2].astype(jnp.bfloat16), "blk", axis=0, tiled=True).astype(
            jnp.float32
        ),
        lax.all_gather(summed[3].astype(jnp.bfloat16), "blk", axis=0, tiled=True).astype(
            jnp.float32
        ),
        lax.all_gather(summed[4].astype(jnp.bfloat16), "blk", axis=0, tiled=True).astype(
            jnp.float32
        ),
        lax.all_gather(summed[5].astype(jnp.bfloat16), "blk", axis=0, tiled=True).astype(
            jnp.float32
        ),
        lax.all_gather(summed[6].astype(jnp.bfloat16), "blk", axis=0, tiled=True).astype(
            jnp.float32
        ),
        lax.all_gather(summed[7].astype(jnp.bfloat16), "blk", axis=0, tiled=True).astype(
            jnp.float32
        ),
        lax.all_gather(summed[8].astype(jnp.bfloat16), "blk", axis=0, tiled=True).astype(
            jnp.float32
        ),
        lax.all_gather(summed[9].astype(jnp.bfloat16), "blk", axis=0, tiled=True).astype(
            jnp.float32
        ),
        lax.all_gather(summed[10].astype(jnp.bfloat16), "blk", axis=0, tiled=True).astype(
            jnp.float32
        ),
        lax.all_gather(summed[11].astype(jnp.bfloat16), "blk", axis=0, tiled=True).astype(
            jnp.float32
        ),
        lax.all_gather(summed[12].astype(jnp.bfloat16), "blk", axis=0, tiled=True).astype(
            jnp.float32
        ),
    )


def local(
    tokens,
    counts,
    ln1_gain,
    ln1_shift,
    w_qkv,
    bias_q,
    bias_v,
    w_out,
    bias_out,
    ln2_gain,
    ln2_shift,
    w_fc1,
    bias_fc1,
    w_fc2,
    bias_fc2,
    cotangent,
):
    cube_count, row_count, width = tokens.shape
    head_count = HEADS
    depth = HD
    score_scale = HD ** (-0.5)
    inputs = tokens.astype(jnp.float32)
    gain_one = ln1_gain.astype(jnp.float32)
    shift_one = ln1_shift.astype(jnp.float32)
    gain_two = ln2_gain.astype(jnp.float32)
    shift_two = ln2_shift.astype(jnp.float32)
    normed = norm_rows(inputs, gain_one, shift_one).astype(jnp.bfloat16)
    project = jnp.dot(normed, w_qkv, preferred_element_type=jnp.float32)
    queries = (project[..., :width] + bias_q.astype(jnp.float32)).astype(jnp.bfloat16)
    key_local = project[..., width : 2 * width].astype(jnp.bfloat16)
    value_local = (project[..., 2 * width :] + bias_v.astype(jnp.float32)).astype(jnp.bfloat16)
    key_all, value_all = (
        lax.all_gather(key_local, "blk", axis=1, tiled=True),
        lax.all_gather(value_local, "blk", axis=1, tiled=True),
    )
    seq_rows = key_all.shape[1]
    block_rows = math.gcd(seq_rows, 512)
    block_count = seq_rows // block_rows
    block_steps = jnp.arange(block_count, dtype=jnp.int32)
    query_heads = queries.reshape(cube_count, row_count, head_count, depth)

    def key_slices(offset):
        key_part = lax.dynamic_slice_in_dim(key_all, offset, block_rows, 1).reshape(
            cube_count, block_rows, head_count, depth
        )
        value_part = lax.dynamic_slice_in_dim(value_all, offset, block_rows, 1).reshape(
            cube_count, block_rows, head_count, depth
        )
        usable = cube_valid(counts, offset, block_rows)[:, None, None, :]
        return (key_part, value_part, usable)

    def forward_block(carry, step_index):
        row_top, row_total, accum = carry
        key_part, value_part, usable = key_slices(step_index * block_rows)
        scores = (
            jnp.einsum("cqhd,ckhd->chqk", query_heads, key_part, preferred_element_type=jnp.float32)
            * score_scale
        )
        masked = jnp.where(usable, scores, MASK_LOW)
        new_top = jnp.maximum(row_top, jnp.max(masked, axis=-1))
        factor = jnp.exp(row_top - new_top)
        weights = jnp.where(usable, jnp.exp(masked - new_top[..., None]), 0.0)
        row_total = row_total * factor + jnp.sum(weights, axis=-1)
        accum = accum * jnp.transpose(factor, (0, 2, 1))[..., None] + jnp.einsum(
            "chqk,ckhd->cqhd",
            weights.astype(jnp.bfloat16),
            value_part,
            preferred_element_type=jnp.float32,
        )
        return ((new_top, row_total, accum), None)

    start_carry = (
        jnp.full((cube_count, head_count, row_count), MASK_LOW, jnp.float32),
        jnp.zeros((cube_count, head_count, row_count), jnp.float32),
        jnp.zeros((cube_count, row_count, head_count, depth), jnp.float32),
    )
    (row_top, row_total, accum), _ = lax.scan(forward_block, start_carry, block_steps)
    attended_f = (accum / jnp.transpose(row_total, (0, 2, 1))[..., None]).reshape(
        cube_count, row_count, width
    )
    log_total = row_top + jnp.log(row_total)
    attended = attended_f.astype(jnp.bfloat16)
    middle = (
        inputs
        + jnp.dot(attended, w_out, preferred_element_type=jnp.float32)
        + bias_out.astype(jnp.float32)
    )
    normed_two = norm_rows(middle, gain_two, shift_two).astype(jnp.bfloat16)
    hidden = jnp.dot(normed_two, w_fc1, preferred_element_type=jnp.float32) + bias_fc1.astype(
        jnp.float32
    )
    active = gelu_exact(hidden).astype(jnp.bfloat16)
    output = (
        middle
        + jnp.dot(active, w_fc2, preferred_element_type=jnp.float32)
        + bias_fc2.astype(jnp.float32)
    ).astype(jnp.bfloat16)
    grad_bias_fc2 = jnp.sum(cotangent.astype(jnp.float32), axis=(0, 1))
    grad_w_fc2 = jnp.einsum("ctf,ctd->fd", active, cotangent, preferred_element_type=jnp.float32)
    back_active = jnp.einsum("ctd,fd->ctf", cotangent, w_fc2, preferred_element_type=jnp.float32)
    _, gelu_pull = jax.vjp(gelu_exact, hidden)
    back_hidden = gelu_pull(back_active)[0]
    grad_bias_fc1 = jnp.sum(back_hidden, axis=(0, 1))
    hidden_low = back_hidden.astype(jnp.bfloat16)
    grad_w_fc1 = jnp.einsum(
        "ctd,ctf->df", normed_two, hidden_low, preferred_element_type=jnp.float32
    )
    back_normed_two = jnp.einsum(
        "ctf,df->ctd", hidden_low, w_fc1, preferred_element_type=jnp.float32
    )
    _, norm_pull_two = jax.vjp(norm_rows, middle, gain_two, shift_two)
    back_middle_norm, grad_ln2_gain, grad_ln2_shift = norm_pull_two(back_normed_two)
    back_middle = cotangent.astype(jnp.float32) + back_middle_norm
    mlp_grads = (
        grad_ln2_gain,
        grad_ln2_shift,
        grad_w_fc1,
        grad_bias_fc1,
        grad_w_fc2,
        grad_bias_fc2,
    )
    grad_bias_out = jnp.sum(back_middle, axis=(0, 1))
    middle_low = back_middle.astype(jnp.bfloat16)
    grad_w_out = jnp.einsum("ctd,cte->de", attended, middle_low, preferred_element_type=jnp.float32)
    back_attended = jnp.einsum(
        "cte,de->ctd", middle_low, w_out, preferred_element_type=jnp.float32
    ).astype(jnp.bfloat16)
    back_heads = back_attended.reshape(cube_count, row_count, head_count, depth)
    delta = jnp.transpose(
        jnp.sum(
            (back_attended.astype(jnp.float32) * attended_f).reshape(
                cube_count, row_count, head_count, depth
            ),
            axis=-1,
        ),
        (0, 2, 1),
    )

    def block_grads(key_part, value_part, usable):
        scores = (
            jnp.einsum("cqhd,ckhd->chqk", query_heads, key_part, preferred_element_type=jnp.float32)
            * score_scale
        )
        probs = jnp.where(usable, jnp.exp(scores - log_total[..., None]), 0.0)
        back_probs = jnp.einsum(
            "cqhd,ckhd->chqk", back_heads, value_part, preferred_element_type=jnp.float32
        )
        back_scores = (probs * (back_probs - delta[..., None])).astype(jnp.bfloat16)
        return (probs, back_scores)

    query_zero = jnp.zeros((cube_count, row_count, head_count, depth), jnp.float32)

    def back_block(carry, step_index):
        back_query, key_grads, value_grads = carry
        offset = step_index * block_rows
        key_part, value_part, usable = key_slices(offset)
        probs, back_scores = block_grads(key_part, value_part, usable)
        back_query = (
            back_query
            + jnp.einsum(
                "chqk,ckhd->cqhd", back_scores, key_part, preferred_element_type=jnp.float32
            )
            * score_scale
        )
        key_block = (
            jnp.einsum(
                "chqk,cqhd->ckhd", back_scores, query_heads, preferred_element_type=jnp.float32
            )
            * score_scale
        )
        value_block = jnp.einsum(
            "chqk,cqhd->ckhd",
            probs.astype(jnp.bfloat16),
            back_heads,
            preferred_element_type=jnp.float32,
        )
        key_grads = lax.dynamic_update_slice_in_dim(
            key_grads, key_block.reshape(cube_count, block_rows, width), offset, 1
        )
        value_grads = lax.dynamic_update_slice_in_dim(
            value_grads, value_block.reshape(cube_count, block_rows, width), offset, 1
        )
        return ((back_query, key_grads, value_grads), None)

    full_zero = jnp.zeros((cube_count, seq_rows, width), jnp.float32)
    (back_query, key_grads, value_grads), _ = lax.scan(
        back_block, (query_zero, full_zero, full_zero), block_steps
    )
    key_back, value_back = (
        lax.psum_scatter(
            key_grads.astype(jnp.bfloat16), "blk", scatter_dimension=1, tiled=True
        ).astype(jnp.float32),
        lax.psum_scatter(
            value_grads.astype(jnp.bfloat16), "blk", scatter_dimension=1, tiled=True
        ).astype(jnp.float32),
    )
    query_low = back_query.reshape(cube_count, row_count, width).astype(jnp.bfloat16)
    key_low = key_back.astype(jnp.bfloat16)
    value_low = value_back.astype(jnp.bfloat16)
    grad_bias_q = jnp.sum(query_low.astype(jnp.float32), axis=(0, 1))
    grad_bias_v = jnp.sum(value_low.astype(jnp.float32), axis=(0, 1))
    back_project = jnp.concatenate([query_low, key_low, value_low], axis=-1)
    grad_w_qkv = jnp.einsum("ctd,cte->de", normed, back_project, preferred_element_type=jnp.float32)
    back_normed = jnp.einsum("cte,de->ctd", back_project, w_qkv, preferred_element_type=jnp.float32)
    _, norm_pull_one = jax.vjp(norm_rows, inputs, gain_one, shift_one)
    back_inputs, grad_ln1_gain, grad_ln1_shift = norm_pull_one(back_normed)
    input_grad = back_middle + back_inputs
    attn_grads = (
        grad_ln1_gain,
        grad_ln1_shift,
        grad_w_qkv,
        grad_bias_q,
        grad_bias_v,
        grad_w_out,
        grad_bias_out,
    )
    every_grad = total_every(attn_grads + mlp_grads)
    attn_grads = every_grad[:7]
    mlp_grads = every_grad[7:]
    return (
        output,
        input_grad,
        attn_grads[0],
        attn_grads[1],
        attn_grads[2],
        attn_grads[3],
        attn_grads[4],
        attn_grads[5],
        attn_grads[6],
        mlp_grads[0],
        mlp_grads[1],
        mlp_grads[2],
        mlp_grads[3],
        mlp_grads[4],
        mlp_grads[5],
    )


def solution(mesh):
    return jax.shard_map(
        local,
        mesh=mesh,
        in_specs=(
            P("dp", "blk", None),
            P("dp"),
            P(),
            P(),
            P(),
            P(),
            P(),
            P(),
            P(),
            P(),
            P(),
            P(),
            P(),
            P(),
            P(),
            P("dp", "blk", None),
        ),
        out_specs=(
            P("dp", "blk", None),
            P("dp", "blk", None),
            P(),
            P(),
            P(),
            P(),
            P(),
            P(),
            P(),
            P(),
            P(),
            P(),
            P(),
            P(),
            P(),
        ),
        check_vma=False,
    )
```

profile of v0, /device:TPU:0, one launch (start us, length us, event | category | flops | bytes accessed | tf_op | source)
XLA Modules:
  0.0 1723.7 jit_solution(9099877610742859206)
XLA Ops:
  15.7 4.7 fusion.50
  36.6 120.0 %all-gather.10.cloned.1.call-done = bf16[3,1536,768]{2,1,0:T(8,128)(2,1)} async-done(((bf16[3,384,768]{2,1,0:T(8,128)(2,1)}), bf16[3,1536,768]{2,1,0:T(8,128)(2,1)}) %all-gather.10.cloned.1.call-update) | async-done | bytes 7077904 | tf_op jit(solution)/shard_map/all_gather | solution.py:165
  156.7 10.4 copy.66
  167.1 118.2 %all-gather.8.cloned.1.call-done = bf16[3,1536,768]{2,1,0:T(8,128)(2,1)} async-done(((bf16[3,384,768]{2,1,0:T(8,128)(2,1)}), bf16[3,1536,768]{2,1,0:T(8,128)(2,1)}) %all-gather.8.cloned.1.call-update) | async-done | bytes 7077904 | tf_op jit(solution)/shard_map/all_gather | solution.py:164
  285.2 10.3 copy.65
  295.5 142.2 %while.30 = (s32[]{:T(128)}, f32[3,12,384]{2,1,0:T(8,128)}, f32[3,12,384]{2,1,0:T(8,128)}, f32[3,384,12,64]{1,3,2,0:T(8,128)}, s32[3]{0:T(128)S(1)}, /*index=5*/...) while((s32[]{:T(128)}, f32[3,12,384]{2,1,0:T(8,128)}, ...), condition=%wide.region_5.6_spmd.clone, body=%wide.region_2.5_spmd.clone.sunk | while | flops 1906691072 | bytes 116574536 | solution.py:208
  299.7 13.2 bitcast_reduce_fusion.2
  313.0 14.0 fusion.123
  327.0 14.5 bitcast_add_fusion.4
  346.5 13.2 bitcast_reduce_fusion.2
  359.7 14.0 fusion.123
  373.7 15.5 bitcast_add_fusion.4
  394.2 13.2 bitcast_reduce_fusion.2
  407.4 14.0 fusion.123
  421.5 15.5 bitcast_add_fusion.4
  443.3 5.3 copy.69
  448.7 4.8 fusion.76
  454.3 15.4 fusion.55
  469.7 35.1 %multiply_convert_fusion.1 = (bf16[3,384,3072]{2,1,0:T(8,128)(2,1)}, f32[3,384,3072]{2,1,0:T(8,128)}) fusion(f32[3,384,3072]{2,1,0:T(8,128)} %get-tuple-element.369, f32[3072]{0:T(1024)S(1)} %copy-done.34, u8[384,3072]{1,0:T(8,128)(4,1)S(1)} %get-tuple-element.267, u8[384,3072]{1,0:T(8,128)(4,1)S(1)} %get-tuple-element.266), kind=kLoop, calls=%fused_computation.47 | loop fusion | flops 251265024 | bytes 37761024 | tf_op jit(solution)/shard_map/convert_element_type | solution.py:223
  504.9 19.3 %fusion.77 = (bf16[3072]{0:T(1024)(128)(2,1)}, bf16[3,384,3072]{2,1,0:T(8,128)(2,1)}) fusion(f32[3,384,3072]{2,1,0:T(8,128)} %get-tuple-element.354, bf16[3,384,768]{2,1,0:T(8,128)(2,1)} %param.35, bf16[3072,768]{1,0:T(8,128)(2,1)} %param.33, f32[3,384,3072]{2,1,0:T(8,128)} %get-tuple-element.369, f32[3072]{0:T(1024)} %convert_element_type.233), kind=kOutput, calls=%fused_computation.137 | convolution fusion | flops 5492438016 | bytes 41895936 | tf_op jit(solution)/shard_map/ctd,fd->ctf/dot_general | solution.py:231
  524.1 12.8 multiply_reduce_fusion
  546.5 5.1 copy.70
  565.1 258.4 %while.31 = (s32[]{:T(128)}, f32[3,384,12,64]{1,3,2,0:T(8,128)}, bf16[3,1536,768]{2,1,0:T(8,128)(2,1)}, bf16[3,1536,768]{2,1,0:T(8,128)(2,1)}, s32[3]{0:T(128)S(...) while((s32[]{:T(128)}, f32[3,384,12,64]{1,3,2,0:T(8,128)}, ...), condition=%wide.region_12.13_spmd.clone, body=%wide.region_11.12_spmd.clone.sunk | while | flops 4605642752 | bytes 262499248 | solution.py:317
  573.2 11.4 fusion.135
  584.5 13.8 fusion.136
  598.4 21.6 %multiply_convert_fusion.3 = bf16[3,12,512,384]{3,2,1,0:T(8,128)(2,1)} fusion(f32[3,12,512,384]{3,2,1,0:T(8,128)} %fusion.135, f32[3,12,384]{2,1,0:T(8,128)S(1)} %copy-done.23, f32[3,12,384]{2,1,0:T(8,128)S(1)} %copy-done.22, pred[3,512]{1,0:T(4,128)(4,1)S(1)} %broadcast_compare_fusion.5, bf16[3,512,12,64]{1,3,2,0:T(8,128)(2,1)} %bitcast.161, ...), kind=kOutput, calls=%fused_computation.24.clone.1 | convolution fusion | flops 948436992 | bytes 46708224 | tf_op jit(solution)/shard_map/while/body/eval_jaxpr/cqhd,ckhd->chqk/dot_general | solution.py:276
  624.3 10.2 bitcast_add_fusion.5
  635.8 5.7 broadcast_multiply_fusion.4
  645.7 4.8 constant_dynamic-update-slice_fusion.3
  658.4 11.4 fusion.135
  669.8 13.8 fusion.136
  683.6 21.6 %multiply_convert_fusion.3 = bf16[3,12,512,384]{3,2,1,0:T(8,128)(2,1)} fusion(f32[3,12,512,384]{3,2,1,0:T(8,128)} %fusion.135, f32[3,12,384]{2,1,0:T(8,128)S(1)} %copy-done.23, f32[3,12,384]{2,1,0:T(8,128)S(1)} %copy-done.22, pred[3,512]{1,0:T(4,128)(4,1)S(1)} %broadcast_compare_fusion.5, bf16[3,512,12,64]{1,3,2,0:T(8,128)(2,1)} %bitcast.161, ...), kind=kOutput, calls=%fused_computation.24.clone.1 | convolution fusion | flops 948436992 | bytes 46708224 | tf_op jit(solution)/shard_map/while/body/eval_jaxpr/cqhd,ckhd->chqk/dot_general | solution.py:276
  709.5 11.3 bitcast_add_fusion.5
  722.0 5.7 broadcast_multiply_fusion.4
  732.0 4.8 constant_dynamic-update-slice_fusion.3
  744.7 11.4 fusion.135
  756.1 13.8 fusion.136
  770.0 21.6 %multiply_convert_fusion.3 = bf16[3,12,512,384]{3,2,1,0:T(8,128)(2,1)} fusion(f32[3,12,512,384]{3,2,1,0:T(8,128)} %fusion.135, f32[3,12,384]{2,1,0:T(8,128)S(1)} %copy-done.23, f32[3,12,384]{2,1,0:T(8,128)S(1)} %copy-done.22, pred[3,512]{1,0:T(4,128)(4,1)S(1)} %broadcast_compare_fusion.5, bf16[3,512,12,64]{1,3,2,0:T(8,128)(2,1)} %bitcast.161, ...), kind=kOutput, calls=%fused_computation.24.clone.1 | convolution fusion | flops 948436992 | bytes 46708224 | tf_op jit(solution)/shard_map/while/body/eval_jaxpr/cqhd,ckhd->chqk/dot_general | solution.py:276
  795.8 11.3 bitcast_add_fusion.5
  808.3 5.7 broadcast_multiply_fusion.4
  818.3 4.8 constant_dynamic-update-slice_fusion.3
  824.2 5.3 bitcast_convert_fusion.3
  829.5 10.6 bitcast_convert_fusion
  840.8 12.0 bitcast_convert_fusion.1
  860.7 84.6 %reduce-scatter.9.cloned.1.call-done = bf16[3,384,768]{2,1,0:T(8,128)(2,1)} async-done(((bf16[3,1536,768]{2,1,0:T(8,128)(2,1)}), bf16[3,384,768]{2,1,0:T(8,128)(2,1)}) %reduce-scatter.9.cloned.1.call-update) | async-done | bytes 1769488 | tf_op jit(solution)/shard_map/reduce_scatter | solution.py:324
  945.4 126.2 %reduce-scatter.7.cloned.1.call-done = bf16[3,384,768]{2,1,0:T(8,128)(2,1)} async-done(((bf16[3,1536,768]{2,1,0:T(8,128)(2,1)}), bf16[3,384,768]{2,1,0:T(8,128)(2,1)}) %reduce-scatter.7.cloned.1.call-update) | async-done | bytes 1769488 | tf_op jit(solution)/shard_map/reduce_scatter | solution.py:321
  1071.6 10.0 bitcast_convert_fusion.2
  1081.6 21.8 %reduce-scatter.13.cloned.1.call-done = bf16[192,768]{1,0:T(8,128)(2,1)} async-done(((bf16[768,768]{1,0:T(8,128)(2,1)}), bf16[192,768]{1,0:T(8,128)(2,1)}) %reduce-scatter.13.cloned.1.call-update) | async-done | bytes 294928 | tf_op jit(solution)/shard_map/reduce_scatter | solution.py:48
  1103.4 86.8 %reduce-scatter.17.cloned.1.call-done = bf16[768,768]{1,0:T(8,128)(2,1)} async-done(((bf16[3072,768]{1,0:T(8,128)(2,1)}), bf16[768,768]{1,0:T(8,128)(2,1)}) %reduce-scatter.17.cloned.1.call-update) | async-done | bytes 1179664 | tf_op jit(solution)/shard_map/reduce_scatter | solution.py:66
  1190.2 88.7 %reduce-scatter.15.cloned.1.call-done = bf16[192,3072]{1,0:T(8,128)(2,1)} async-done(((bf16[768,3072]{1,0:T(8,128)(2,1)}), bf16[192,3072]{1,0:T(8,128)(2,1)}) %reduce-scatter.15.cloned.1.call-update) | async-done | bytes 1179664 | tf_op jit(solution)/shard_map/reduce_scatter | solution.py:60
  1278.9 69.8 %reduce-scatter.11.cloned.1.call-done = bf16[192,2304]{1,0:T(8,128)(2,1)} async-done(((bf16[768,2304]{1,0:T(8,128)(2,1)}), bf16[192,2304]{1,0:T(8,128)(2,1)}) %reduce-scatter.11.cloned.1.call-update) | async-done | bytes 884752 | tf_op jit(solution)/shard_map/reduce_scatter | solution.py:39
  1348.7 78.3 %all-reduce.23.cloned.1.call-done = (bf16[192,2304]{1,0:T(8,128)(2,1)}, bf16[192,768]{1,0:T(8,128)(2,1)}, bf16[192,3072]{1,0:T(8,128)(2,1)}, bf16[768,768]{1,0:T(8,128)(2,1)}) async-done(((bf16[192,2304]{1,0:T(8,128)(2,1)}, bf16[192,768]{1,0:T(8,128)(2,1)}, bf16[192,3072]{1,0:T(8,128)(2,1)}, bf16[768,768]{1,0:T(8,128)(2,1)}), (bf16[192,2304]{1,0:T(8,128)(2,1)}, bf16[192,768]{1,0:T(8,128)(2,1)}, ...) | async-done | bytes 3538960 | tf_op jit(solution)/shard_map/psum | solution.py:76
  1437.5 10.9 add_convert_fusion
  1450.8 8.6 fusion.71
  1461.8 20.9 %all-reduce.20 = (bf16[768]{0:T(1024)(128)(2,1)}, bf16[768]{0:T(1024)(128)(2,1)}, bf16[768]{0:T(1024)(128)(2,1)}, bf16[768]{0:T(1024)(128)(2,1)}, bf16[768]{0:T(...) all-reduce(bf16[768]{0:T(1024)(128)(2,1)} %get-tuple-element.270, ...), channel_id=4, replica_groups=mesh['dp'=8,'blk'=4] {'blk'}, use_global_device_ids=true, to_apply=%region_18.19.clone | all-reduce | flops 9216 | bytes 36864
  1494.2 13.5 all-reduce.17
  1523.2 16.8 all-reduce.19
  1550.9 14.0 all-gather
  1566.2 6.3 add_add_fusion.2
  1575.4 5.5 convert_element_type.251
  1580.9 39.2 %all-gather.18.cloned.1.call-done = bf16[3072,768]{1,0:T(8,128)(2,1)} async-done(((bf16[768,768]{1,0:T(8,128)(2,1)}), bf16[3072,768]{1,0:T(8,128)(2,1)}) %all-gather.18.cloned.1.call-update) | async-done | bytes 4718608 | tf_op jit(solution)/shard_map/all_gather | solution.py:122
  1620.1 6.8 convert_element_type.267
  1626.9 82.7 %all-gather.16.cloned.1.call-done = bf16[768,3072]{1,0:T(8,128)(2,1)} async-done(((bf16[192,3072]{1,0:T(8,128)(2,1)}), bf16[768,3072]{1,0:T(8,128)(2,1)}) %all-gather.16.cloned.1.call-update) | async-done | bytes 4718608 | tf_op jit(solution)/shard_map/all_gather | solution.py:116
  1709.6 7.4 convert_element_type.263
  (287 shorter events, 182.6 us)
Async XLA Ops:
  7.2 8.6 copy-start
  7.2 149.5 %all-gather.10.cloned.1.call-start = ((), (), s32[]{:S(2)}) async-start(), calls=%async_computation.7 | async-start | bytes 8847360 | tf_op jit(solution)/shard_map/all_gather | solution.py:165
  7.2 8.5 copy-start.7
  8.1 7.0 copy-start.35
  9.2 5.9 copy-start.43
  12.4 2.7 copy-start.20
  20.4 5.1 copy-start.15
  25.6 4.1 copy-start.46
  25.6 4.7 copy-start.47
  25.6 6.6 copy-start.42
  25.6 259.6 %all-gather.8.cloned.1.call-start = ((), (), s32[]{:S(2)}) async-start(), calls=%async_computation.6 | async-start | bytes 8847360 | tf_op jit(solution)/shard_map/all_gather | solution.py:164
  29.0 916.3 %reduce-scatter.9.cloned.1.call-start = ((), (), s32[]{:S(2)}) async-start(), calls=%async_computation.9 | async-start | bytes 8847360 | tf_op jit(solution)/shard_map/reduce_scatter | solution.py:324
  167.1 128.4 %copy-start.32 = (s32[3]{0:T(128)S(1)}, s32[3]{0:T(128)}, u32[]{:S(2)}) copy-start(s32[3]{0:T(128)} %param.21) | copy-start | bytes 40
  296.8 2.9 copy-start.3
  299.7 13.2 copy-start.14
  327.0 14.5 copy-start.17
  343.5 2.9 copy-start.3
  346.5 13.2 copy-start.14
  373.7 15.5 copy-start.17
  391.2 2.9 copy-start.3
  394.2 13.2 copy-start.14
  421.4 15.5 copy-start.17
  443.3 5.3 copy-start.45
  453.5 16.3 copy-start.11
  453.5 83.4 %copy-start.27 = (f32[3,384]{1,0:T(4,128)}, f32[3,384]{1,0:T(4,128)S(1)}, u32[]{:S(2)}) copy-start(f32[3,384]{1,0:T(4,128)S(1)} %broadcast_multiply_fusion.1) | copy-start | bytes 13828
  454.3 15.4 copy-start.37
  524.1 12.8 copy-start.12
  524.1 12.8 copy-start.38
  524.1 12.8 copy-start.41
  538.5 3.7 copy-start.10
  538.5 4.0 copy-start.19
  540.0 6.5 copy-start.16
  561.8 3.3 copy-start.33
  569.8 3.4 copy-start.4
  573.2 11.4 copy-start.22
  584.5 13.8 copy-start.23
  624.3 10.5 copy-start.1
  624.3 11.5 copy-start.5
  655.0 3.4 copy-start.4
  658.4 11.4 copy-start.22
  669.8 13.8 copy-start.23
  709.5 11.5 copy-start.1
  709.5 12.5 copy-start.5
  741.4 3.4 copy-start.4
  744.7 11.4 copy-start.22
  756.1 13.8 copy-start.23
  795.8 11.5 copy-start.1
  795.8 12.5 copy-start.5
  823.6 248.0 %reduce-scatter.7.cloned.1.call-start = ((), (), s32[]{:S(2)}) async-start(), calls=%async_computation.8 | async-start | bytes 8847360 | tf_op jit(solution)/shard_map/reduce_scatter | solution.py:321
  824.1 279.3 %reduce-scatter.13.cloned.1.call-start = ((), (), s32[]{:S(2)}) async-start(), calls=%async_computation.12 | async-start | bytes 1474560 | tf_op jit(solution)/shard_map/reduce_scatter | solution.py:48
  829.5 360.7 %reduce-scatter.17.cloned.1.call-start = ((), (), s32[]{:S(2)}) async-start(), calls=%async_computation.16 | async-start | bytes 5898240 | tf_op jit(solution)/shard_map/reduce_scatter | solution.py:66
  840.1 438.8 %reduce-scatter.15.cloned.1.call-start = ((), (), s32[]{:S(2)}) async-start(), calls=%async_computation.14 | async-start | bytes 5898240 | tf_op jit(solution)/shard_map/reduce_scatter | solution.py:60
  852.8 495.9 %reduce-scatter.11.cloned.1.call-start = ((), (), s32[]{:S(2)}) async-start(), calls=%async_computation.10 | async-start | bytes 4423680 | tf_op jit(solution)/shard_map/reduce_scatter | solution.py:39
  852.9 218.7 %copy-start.21 = (f32[3,384]{1,0:T(4,128)S(1)}, f32[3,384]{1,0:T(4,128)}, u32[]{:S(2)}) copy-start(f32[3,384]{1,0:T(4,128)} %copy-done.20) | copy-start | bytes 13828
  852.9 218.7 %copy-start.25 = (f32[3,384]{1,0:T(4,128)S(1)}, f32[3,384]{1,0:T(4,128)}, u32[]{:S(2)}) copy-start(f32[3,384]{1,0:T(4,128)} %copy-done.24) | copy-start | bytes 13828
  1081.6 345.5 %all-reduce.23.cloned.1.call-start = ((), (), s32[]{:S(2)}) async-start(), calls=%async_computation.18 | async-start | bytes 7077888 | tf_op jit(solution)/shard_map/psum | solution.py:76
  1348.7 223.8 %all-gather.14.cloned.1.call-start = ((), (), s32[]{:S(2)}) async-start(), calls=%async_computation.13 | async-start | bytes 1474560 | tf_op jit(solution)/shard_map/all_gather | solution.py:104
  1427.1 148.3 %all-gather.12.cloned.1.call-start = ((), (), s32[]{:S(2)}) async-start(), calls=%async_computation.11 | async-start | bytes 4423680 | tf_op jit(solution)/shard_map/all_gather | solution.py:95
  1427.8 192.2 %all-gather.18.cloned.1.call-start = ((), (), s32[]{:S(2)}) async-start(), calls=%async_computation.17 | async-start | bytes 5898240 | tf_op jit(solution)/shard_map/all_gather | solution.py:122
  1428.4 281.2 %all-gather.16.cloned.1.call-start = ((), (), s32[]{:S(2)}) async-start(), calls=%async_computation.15 | async-start | bytes 5898240 | tf_op jit(solution)/shard_map/all_gather | solution.py:116
  1450.8 8.6 copy-start.31
  1450.8 8.6 copy-start.8
  1450.8 8.6 copy-start.36
  1459.4 2.4 copy-start.13
  (17 other events, 18.5 us)
Sparse Core Ops, SparseCore 0:
  25.7 130.8 all-gather.9
  158.8 126.3 all-gather.7
  823.7 121.6 reduce-scatter.8
  947.5 123.9 reduce-scatter.6
  1073.7 29.6 reduce-scatter.12
  1106.2 83.9 reduce-scatter.16
  1193.1 85.7 reduce-scatter.14
  1281.8 66.8 reduce-scatter.10
  1352.4 74.6 all-reduce.22
  1428.5 30.5 all-gather.13
  1460.6 69.8 all-gather.11
  1531.9 88.1 all-gather.17
  1621.7 87.8 all-gather.15
where the time goes:
time: 1730 us; the launch traced here: 1720 us
  waiting for transfers between devices  919 us (53%)
  matrix products  394 us (23%)
  local copies, waits for them, and re-layouts  168 us (10%)
  other arithmetic  156 us (9%)
  blocking collectives  65.3 us (4%)
    reduce_scatter x1, waiting for transfers between devices, local(): lax.psum_scatter(key_grads.astype(jnp.bfloat16), 'blk', scatter_dimension...  126 us
    all_gather x1, waiting for transfers between devices, local(): lax.all_gather(value_local, 'blk', axis=1, tiled=True)  120 us
    all_gather x1, waiting for transfers between devices, local(): lax.all_gather(key_local, 'blk', axis=1, tiled=True)  118 us
    reduce_scatter x1, waiting for transfers between devices, total_every(): lax.psum_scatter(parts[9].astype(jnp.bfloat16), 'blk', scatter_dimension=...  88.7 us
    reduce_scatter x1, waiting for transfers between devices, total_every(): lax.psum_scatter(parts[11].astype(jnp.bfloat16), 'blk', scatter_dimension...  86.8 us
    reduce_scatter x1, waiting for transfers between devices, local(): lax.psum_scatter(value_grads.astype(jnp.bfloat16), 'blk', scatter_dimensi...  84.6 us
    all_gather x1, waiting for transfers between devices, total_every(): lax.all_gather(summed[9].astype(jnp.bfloat16), 'blk', axis=0, tiled=True)  82.7 us
    psum x1, waiting for transfers between devices, total_every(): lax.psum(split[2].astype(jnp.bfloat16), 'dp').astype(jnp.float32)  78.3 us
  transfers between devices with their start and end apart: 13, of which 11 were waited for; matrix products, arithmetic and copies ran while one was open for 9% of the time, Pallas kernels for 0%

commit v1 on v0

--- a/solution.py
+++ b/solution.py
@@ -1,12 +1,16 @@
+import functools
 import math
 
 import jax
 import jax.numpy as jnp
 from jax import lax
+from jax.experimental import pallas as pl
+from jax.experimental.pallas import tpu as pltpu
 from jax.sharding import PartitionSpec as P
 
 HEADS = 12
 HD = 64
+SHORT = 864
 
 
 NORM_EPS = 1e-06
@@ -367,9 +371,637 @@
     )
 
 
+F32 = jnp.float32
+BF16 = jnp.bfloat16
+EXP_SCALE = math.log2(math.e) / 8
+LANES = 128
+VMEM = pl.BlockSpec(memory_space=pltpu.VMEM)
+
+
+def shape_of(shape, dtype):
+    return jax.ShapeDtypeStruct(shape, dtype)
+
+
+def limits(mib):
+    return pltpu.CompilerParams(vmem_limit_bytes=mib * 2**20)
+
+
+def dot_nt(a, b):
+    return lax.dot_general(a, b, (((1,), (1,)), ((), ())), preferred_element_type=F32)
+
+
+def dot_nn(a, b):
+    return lax.dot_general(a, b, (((1,), (0,)), ((), ())), preferred_element_type=F32)
+
+
+def dot_tn(a, b):
+    return lax.dot_general(a, b, (((0,), (0,)), ((), ())), preferred_element_type=F32)
+
+
+def centred(values):
+    centre = values - jnp.mean(values, axis=1, keepdims=True)
+    spread = jnp.mean(centre * centre, axis=1, keepdims=True)
+    return centre, lax.rsqrt(spread + NORM_EPS)
+
+
+def norm_back(centre, recip, back, gain):
+    unit = centre * recip
+    grad = back * gain
+    inner = jnp.mean(grad * unit, axis=1, keepdims=True)
+    return unit, recip * (grad - jnp.mean(grad, axis=1, keepdims=True) - unit * inner)
+
+
+def project_kernel(*refs, pieces):
+    xs = refs[:pieces]
+    vecs, w, q_ref, kv_ref = refs[pieces:]
+    rows = xs[0].shape[0]
+    gain, shift, bias_q, bias_v = (vecs[i : i + 1, :] for i in range(4))
+    for i in range(pieces):
+        centre, recip = centred(xs[i][...].astype(F32))
+        normed = (centre * recip * gain + shift).astype(BF16)
+        at = pl.ds(i * rows, rows)
+        q_ref[at, :] = (dot_nn(normed, w[:, :768]) + bias_q).astype(BF16)
+        kv_ref[0, at, :] = dot_nn(normed, w[:, 768:1536]).astype(BF16)
+        kv_ref[1, at, :] = (dot_nn(normed, w[:, 1536:]) + bias_v).astype(BF16)
+
+
+def project(xs, vecs, w):
+    n = sum(x.shape[0] for x in xs)
+    return pl.pallas_call(
+        functools.partial(project_kernel, pieces=len(xs)),
+        in_specs=[VMEM] * (len(xs) + 2),
+        out_specs=[VMEM] * 2,
+        out_shape=[shape_of((n, 768), BF16), shape_of((2, n, 768), BF16)],
+        compiler_params=limits(40),
+        cost_estimate=pl.CostEstimate(
+            flops=2 * n * 768 * 2304, bytes_accessed=n * 768 * 8 + 768 * 2304 * 2, transcendentals=0
+        ),
+        name="project",
+    )(*xs, vecs, w)
+
+
+def three_parts(values, lane):
+    high = values.astype(BF16)
+    rest = values - high.astype(F32)
+    middle = rest.astype(BF16)
+    least = (rest - middle.astype(F32)).astype(BF16)
+    zero = jnp.zeros((), BF16)
+    return jnp.where(
+        lane == 0, high, jnp.where(lane == 1, middle, jnp.where(lane == 2, least, zero))
+    )
+
+
+def lane_index(rows=1):
+    return lax.broadcasted_iota(jnp.int32, (rows, LANES), 1)
+
+
+def attend_kernel(*refs, pieces, valid, step):
+    q_ref = refs[0]
+    kvs = refs[1 : 1 + pieces]
+    o_ref, t_ref = refs[1 + pieces :]
+    lane = lane_index()
+    low = lane < 64
+    half = lane % 64
+    total = sum(kv.shape[1] for kv in kvs)
+    keys, values = [], []
+    for h in range(2):
+        own = low if h == 0 else ~low
+        key_parts, value_parts, at = [], [], 0
+        for kv in kvs:
+            n = kv.shape[1]
+            beside = jnp.zeros((n, LANES), BF16)
+            if at + n > valid:
+                place = lax.broadcasted_iota(jnp.int32, (n, LANES), 0) + at
+                beside = jnp.where(
+                    (place >= valid) & (lane_index(n) % 64 == 0), MASK_LOW, 0.0
+                ).astype(BF16)
+            key_parts.append(jnp.where(own, kv[0], beside))
+            value_parts.append(jnp.where(own, kv[1], jnp.ones((), BF16)))
+            at += n
+        keys.append(key_parts)
+        values.append(value_parts)
+    for s in range(q_ref.shape[0] // step):
+        at = pl.ds(s * step, step)
+        q = q_ref[at, :]
+        sums, tops = [], []
+        for h in range(2):
+            own = low if h == 0 else ~low
+            q_own = q
+            if total > valid:
+                q_own = jnp.where(own, q, jnp.where(half == 0, 1.0, 0.0).astype(BF16))
+            scores = [dot_nt(q_own, k) for k in keys[h]]
+            top = functools.reduce(
+                jnp.maximum, [jnp.max(x, axis=1, keepdims=True) for x in scores]
+            )
+            scaled_top = top * EXP_SCALE
+            weights = [jnp.exp2(x * EXP_SCALE - scaled_top).astype(BF16) for x in scores]
+            sums.append(
+                functools.reduce(jnp.add, [dot_nn(p, v) for p, v in zip(weights, values[h])])
+            )
+            tops.append(top)
+        above = jnp.where(low, sums[0], sums[1])
+        below = jnp.where(low, sums[1], sums[0])
+        o_ref[at, :] = above / pltpu.roll(below, 64, 1)
+        log_total = -(jnp.where(low, tops[1], tops[0]) + 8.0 * jnp.log(below))
+        t_ref[at, :] = jnp.where(half == 3, jnp.ones((), BF16), three_parts(log_total, half))
+
+
+def attend(q, kvs, valid, rows, step):
+    n = q.shape[0]
+    keys = sum(kv.shape[1] for kv in kvs)
+    block = pl.BlockSpec((rows, LANES), lambda p, i: (i, p))
+    return pl.pallas_call(
+        functools.partial(attend_kernel, pieces=len(kvs), valid=valid, step=step),
+        out_shape=[shape_of((n, 768), F32), shape_of((n, 768), BF16)],
+        grid=(6, n // rows),
+        in_specs=[block]
+        + [pl.BlockSpec((2, kv.shape[1], LANES), lambda p, i: (0, 0, p)) for kv in kvs],
+        out_specs=[block, block],
+        compiler_params=limits(56),
+        cost_estimate=pl.CostEstimate(
+            flops=16 * n * keys * 768, bytes_accessed=n * 768 * 8, transcendentals=n * keys * 12
+        ),
+        name="attend",
+    )(q, *kvs)
+
+
+def attend_back_kernel(*refs, pieces, valid, step):
+    q_ref, do_ref, o_ref, t_ref = refs[:4]
+    kvs = refs[4 : 4 + pieces]
+    dq_ref = refs[4 + pieces]
+    dkvs = refs[5 + pieces :]
+    n = q_ref.shape[0]
+    lane = lane_index()
+    low = lane < 64
+    half = lane % 64
+    q, do, t = q_ref[...], do_ref[...], t_ref[...]
+    product = do.astype(F32) * o_ref[...]
+    delta = [
+        jnp.sum(jnp.where(low, product, 0.0), axis=1, keepdims=True),
+        jnp.sum(jnp.where(low, 0.0, product), axis=1, keepdims=True),
+    ]
+    d = three_parts(-jnp.where(low, delta[1], delta[0]), half)
+    queries = [jnp.where(low, q, t), jnp.where(low, t, q)]
+    backs = [jnp.where(low, do, d), jnp.where(low, d, do)]
+    ones = jnp.where(half < 3, 1.0, 0.0).astype(BF16)
+    sums = [jnp.zeros((LANES, n), F32), jnp.zeros((LANES, n), F32)]
+    start = 0
+    for kv, dkv in zip(kvs, dkvs):
+        for first in range(0, kv.shape[1], step):
+            size = min(step, kv.shape[1] - first)
+            at = pl.ds(first, size)
+            key_sums, value_sums = [], []
+            for h in range(2):
+                own = low if h == 0 else ~low
+                beside = ones
+                if start + first + size > valid:
+                    place = lax.broadcasted_iota(jnp.int32, (size, LANES), 0) + (start + first)
+                    wide = lane_index(size) % 64
+                    beside = jnp.where(
+                        wide < 3, 1.0, jnp.where((place >= valid) & (wide == 3), MASK_LOW, 0.0)
+                    ).astype(BF16)
+                key = jnp.where(own, kv[0, at, :], beside)
+                value = jnp.where(own, kv[1, at, :], ones)
+                probs = jnp.exp2(dot_nt(key, queries[h]) * EXP_SCALE)
+                back_scores = (probs * dot_nt(value, backs[h])).astype(BF16)
+                value_sums.append(dot_nn(probs.astype(BF16), backs[h]))
+                key_sums.append(dot_nn(back_scores, queries[h]))
+                sums[h] = sums[h] + dot_tn(key, back_scores)
+            dkv[0, at, :] = (jnp.where(low, key_sums[0], key_sums[1]) * 0.125).astype(BF16)
+            dkv[1, at, :] = jnp.where(low, value_sums[0], value_sums[1]).astype(BF16)
+        start += kv.shape[1]
+    both = jnp.concatenate([sums[0][:64], sums[1][64:]], axis=0)
+    dq_ref[...] = (both.T * 0.125).astype(BF16)
+
+
+def attend_back(q, do, o, t, kvs, valid, step):
+    n = q.shape[0]
+    keys = sum(kv.shape[1] for kv in kvs)
+    block = pl.BlockSpec((n, LANES), lambda p: (0, p))
+    wide = [pl.BlockSpec((2, kv.shape[1], LANES), lambda p: (0, 0, p)) for kv in kvs]
+    return pl.pallas_call(
+        functools.partial(attend_back_kernel, pieces=len(kvs), valid=valid, step=step),
+        out_shape=[shape_of((n, 768), BF16)] + [shape_of(kv.shape, BF16) for kv in kvs],
+        grid=(6,),
+        in_specs=[block] * 4 + wide,
+        out_specs=[block] + wide,
+        compiler_params=limits(56),
+        cost_estimate=pl.CostEstimate(
+            flops=40 * n * keys * 768, bytes_accessed=n * 768 * 12, transcendentals=n * keys * 12
+        ),
+        name="attend_back",
+    )(q, do, o, t, *kvs)
+
+
+def feed_kernel(
+    att_full, att_short, x1, x2, x3, c1, c2, c3, w_out, vecs, w1, b1, w2,
+    o1, o2, o3, back_att, back_mid, gw1, gw2, gw_out, gb1, sums,
+    mid, normed, normed_t, out_sum, back_sum, cot, active, hidden_low,
+    *, steps, tile,
+):
+    j = pl.program_id(0)
+    xs, cots, outs = (x1, x2, x3), (c1, c2, c3), (o1, o2, o3)
+    rows = x1.shape[0]
+    full = att_full.shape[0] // rows
+    bias_out, gain, shift, b2 = (vecs[i : i + 1, :] for i in range(4))
+
+    def at(i):
+        return pl.ds(i * rows, rows)
+
+    def attended(i):
+        source = att_full[at(i), :] if i < full else att_short[at(i - full), :]
+        return source.astype(BF16)
+
+    @pl.when(j == 0)
+    def _():
+        for i in range(3):
+            m = xs[i][...].astype(F32) + dot_nn(attended(i), w_out[...]) + bias_out
+            mid[at(i), :] = m
+            centre, recip = centred(m)
+            low = (centre * recip * gain + shift).astype(BF16)
+            normed[at(i), :] = low
+            normed_t[:, at(i)] = low.T
+            cot[at(i), :] = cots[i][...]
+            out_sum[at(i), :] = m + b2
+            back_sum[at(i), :] = jnp.zeros((rows, 768), F32)
+
+    w1_tile, w2_tile = w1[...], w2[...]
+    bias = b1[...]
+    bias_sum = jnp.zeros((1, tile), F32)
+    for i in range(3):
+        h = dot_nn(normed[at(i), :], w1_tile) + bias
+        back_active = dot_nt(cot[at(i), :], w2_tile)
+        share = 0.5 + 0.5 * lax.erf(h * math.sqrt(0.5))
+        act = (h * share).astype(BF16)
+        slope = share + h * (math.sqrt(0.5 / math.pi) * jnp.exp(h * h * (-0.5)))
+        back_hidden = back_active * slope
+        low = back_hidden.astype(BF16)
+        bias_sum = bias_sum + jnp.sum(back_hidden, axis=0, keepdims=True)
+        active[at(i), :] = act
+        hidden_low[at(i), :] = low
+        out_sum[at(i), :] += dot_nn(act, w2_tile)
+        back_sum[at(i), :] += dot_nt(low, w1_tile)
+    gb1[...] = bias_sum
+    gw1[...] = dot_nn(normed_t[...], hidden_low[...]).astype(BF16)
+    gw2[...] = dot_tn(active[...], cot[...]).astype(BF16)
+
+    @pl.when(j == steps - 1)
+    def _():
+        zero = jnp.zeros((1, 768), F32)
+        grad_out, grad_gain, grad_shift, grad_b2 = zero, zero, zero, zero
+        for i in range(3):
+            outs[i][...] = out_sum[at(i), :].astype(BF16)
+            centre, recip = centred(mid[at(i), :])
+            back = back_sum[at(i), :]
+            unit, through = norm_back(centre, recip, back, gain)
+            c = cots[i][...].astype(F32)
+            m = c + through
+            grad_gain = grad_gain + jnp.sum(back * unit, axis=0, keepdims=True)
+            grad_shift = grad_shift + jnp.sum(back, axis=0, keepdims=True)
+            grad_out = grad_out + jnp.sum(m, axis=0, keepdims=True)
+            grad_b2 = grad_b2 + jnp.sum(c, axis=0, keepdims=True)
+            back_mid[at(i), :] = m
+            low = m.astype(BF16)
+            normed[at(i), :] = low
+            back_att[at(i), :] = dot_nt(low, w_out[...]).astype(BF16)
+            cot[at(i), :] = attended(i)
+        gw_out[...] = dot_tn(cot[...], normed[...]).astype(BF16)
+        sums[...] = jnp.concatenate(
+            [grad_out, grad_gain, grad_shift, grad_b2, zero, zero, zero, zero], axis=0
+        )
+
+
+def feed(att_full, att_short, xs, cots, w_out, vecs, w1, b1, w2, tile):
+    rows = xs[0].shape[0]
+    n = rows * 3
+    wide = w1.shape[1]
+    steps = wide // tile
+    across = pl.BlockSpec((768, tile), lambda j: (0, j))
+    down = pl.BlockSpec((tile, 768), lambda j: (j, 0))
+    line = pl.BlockSpec((1, tile), lambda j: (0, j))
+    return pl.pallas_call(
+        functools.partial(feed_kernel, steps=steps, tile=tile),
+        grid=(steps,),
+        in_specs=[VMEM] * 10 + [across, line, down],
+        out_specs=[VMEM] * 5 + [across, down, VMEM, line, VMEM],
+        out_shape=[shape_of((rows, 768), BF16)] * 3
+        + [
+            shape_of((n, 768), BF16),
+            shape_of((n, 768), F32),
+            shape_of((768, wide), BF16),
+            shape_of((wide, 768), BF16),
+            shape_of((768, 768), BF16),
+            shape_of((1, wide), F32),
+            shape_of((8, 768), F32),
+        ],
+        scratch_shapes=[
+            pltpu.VMEM((n, 768), F32),
+            pltpu.VMEM((n, 768), BF16),
+            pltpu.VMEM((768, n), BF16),
+            pltpu.VMEM((n, 768), F32),
+            pltpu.VMEM((n, 768), F32),
+            pltpu.VMEM((n, 768), BF16),
+            pltpu.VMEM((n, tile), BF16),
+            pltpu.VMEM((n, tile), BF16),
+        ],
+        compiler_params=limits(60),
+        cost_estimate=pl.CostEstimate(
+            flops=12 * n * 768 * wide + 6 * n * 768 * 768,
+            bytes_accessed=40 * 2**20,
+            transcendentals=2 * n * wide,
+        ),
+        name="feed",
+    )(att_full, att_short, *xs, *cots, w_out, vecs, w1, b1, w2)
+
+
+def project_grad_kernel(
+    x1, x2, x3, vecs, dq_full, dq_short, own_full, got_full, own_short, got_short,
+    back, gw, sums, normed,
+):
+    rows = x1.shape[0]
+    full = dq_full.shape[0]
+    gain, shift = vecs[0:1, :], vecs[1:2, :]
+    for i, x in enumerate((x1, x2, x3)):
+        centre, recip = centred(x[...].astype(F32))
+        normed[pl.ds(i * rows, rows), :] = (centre * recip * gain + shift).astype(BF16)
+    back[:full, :768] = dq_full[...]
+    back[full:, :768] = dq_short[...]
+    for k in range(2):
+        at = pl.ds(768 * (k + 1), 768)
+        back[:full, at] = (own_full[k].astype(F32) + got_full[k].astype(F32)).astype(BF16)
+        back[full:, at] = (own_short[k].astype(F32) + got_short[k].astype(F32)).astype(BF16)
+    zero = jnp.zeros((6, 768), F32)
+    sums[...] = jnp.concatenate(
+        [
+            jnp.sum(back[:, :768].astype(F32), axis=0, keepdims=True),
+            jnp.sum(back[:, 1536:].astype(F32), axis=0, keepdims=True),
+            zero,
+        ],
+        axis=0,
+    )
+    flipped = normed[...].T
+    for k in range(3):
+        at = pl.ds(768 * k, 768)
+        gw[:, at] = dot_nn(flipped, back[:, at]).astype(BF16)
+
+
+def project_grad(xs, vecs, dq_full, dq_short, own_full, got_full, own_short, got_short):
+    n = sum(x.shape[0] for x in xs)
+    return pl.pallas_call(
+        project_grad_kernel,
+        in_specs=[VMEM] * 10,
+        out_specs=[VMEM] * 3,
+        out_shape=[shape_of((n, 2304), BF16), shape_of((768, 2304), BF16), shape_of((8, 768), F32)],
+        scratch_shapes=[pltpu.VMEM((n, 768), BF16)],
+        compiler_params=limits(56),
+        cost_estimate=pl.CostEstimate(
+            flops=2 * n * 768 * 2304, bytes_accessed=16 * 2**20, transcendentals=0
+        ),
+        name="project_grad",
+    )(*xs, vecs, dq_full, dq_short, own_full, got_full, own_short, got_short)
+
+
+def input_grad_kernel(x1, x2, x3, vecs, back, w, back_mid, o1, o2, o3, sums):
+    rows = x1.shape[0]
+    gain = vecs[0:1, :]
+    zero = jnp.zeros((1, 768), F32)
+    grad_gain, grad_shift = zero, zero
+    for i, (x, out) in enumerate(((x1, o1), (x2, o2), (x3, o3))):
+        at = pl.ds(i * rows, rows)
+        centre, recip = centred(x[...].astype(F32))
+        back_normed = dot_nt(back[at, :], w[...])
+        unit, through = norm_back(centre, recip, back_normed, gain)
+        grad_gain = grad_gain + jnp.sum(back_normed * unit, axis=0, keepdims=True)
+        grad_shift = grad_shift + jnp.sum(back_normed, axis=0, keepdims=True)
+        out[...] = (back_mid[at, :] + through).astype(BF16)
+    sums[...] = jnp.concatenate([grad_gain, grad_shift, jnp.zeros((6, 768), F32)], axis=0)
+
+
+def input_grad_of(xs, vecs, back, w, back_mid):
+    n = back.shape[0]
+    rows = xs[0].shape[0]
+    return pl.pallas_call(
+        input_grad_kernel,
+        in_specs=[VMEM] * 7,
+        out_specs=[VMEM] * 4,
+        out_shape=[shape_of((rows, 768), BF16)] * 3 + [shape_of((8, 768), F32)],
+        compiler_params=limits(56),
+        cost_estimate=pl.CostEstimate(
+            flops=2 * n * 768 * 2304, bytes_accessed=16 * 2**20, transcendentals=0
+        ),
+        name="input_grad",
+    )(*xs, vecs, back, w, back_mid)
+
+
+FIRST_TO = {
+    (0, 0): (0, 0), (0, 1): (0, 1), (0, 2): (1, 0), (0, 3): (1, 1),
+    (1, 0): (0, 2), (1, 1): (0, 3), (1, 2): (1, 2), (1, 3): (1, 3),
+}
+SECOND_TO = {
+    (0, 0): (0, 1), (0, 1): (0, 0), (0, 2): (1, 1), (0, 3): (1, 0),
+    (1, 0): (0, 3), (1, 1): (0, 2), (1, 2): (1, 3), (1, 3): (1, 2),
+}
+
+
+def column_pairs(table):
+    pairs = []
+    for chip in range(4):
+        for (core, z), (core_to, z_to) in table.items():
+            pairs.append(((chip * 2 + core) * 4 + z, (chip * 2 + core_to) * 4 + z_to))
+    return pairs
+
+
+def flip_pairs(size, mask):
+    return [(i, i ^ mask) for i in range(size)]
+
+
+def swap(array, axis, mask):
+    return lax.ppermute(array, axis, flip_pairs(8 if axis == "dp" else 4, mask))
+
+
+def add_low(*terms):
+    return sum(term.astype(F32) for term in terms).astype(BF16)
+
+
+def part_of(array, index, count):
+    rows = array.shape[0] // count
+    return lax.dynamic_slice_in_dim(array, index * rows, rows, 0)
+
+
+class Place:
+    def __init__(self):
+        dp = lax.axis_index("dp")
+        self.z = lax.axis_index("blk")
+        self.core = dp % 2
+        self.chip = dp // 2
+
+
+def sum_apart(arrays, place):
+    halves = []
+    for a in arrays:
+        got = swap(part_of(a, 1 - place.core, 2), "dp", 1)
+        halves.append(add_low(part_of(a, place.core, 2), got))
+    quarters = []
+    for a in halves:
+        got = [swap(part_of(a, place.chip ^ k, 4), "dp", 2 * k) for k in (1, 2, 3)]
+        quarters.append(add_low(part_of(a, place.chip, 4), *got))
+    parts = []
+    for a in quarters:
+        got = [swap(part_of(a, place.z ^ k, 4), "blk", k) for k in (1, 2, 3)]
+        parts.append(add_low(part_of(a, place.z, 4), *got))
+    return parts
+
+
+def spread(piece, got, index):
+    rows = piece.shape[0]
+    whole = jnp.zeros((rows * 4,) + piece.shape[1:], piece.dtype)
+    for k, array in enumerate([piece] + got):
+        whole = lax.dynamic_update_slice_in_dim(whole, array, (index ^ k) * rows, 0)
+    return whole
+
+
+def join(parts, place):
+    wholes = []
+    for a in parts:
+        a = spread(a, [swap(a, "blk", k) for k in (1, 2, 3)], place.z)
+        a = spread(a, [swap(a, "dp", 2 * k) for k in (1, 2, 3)], place.chip)
+        got = swap(a, "dp", 1)
+        first = place.core == 0
+        wholes.append(
+            jnp.concatenate([jnp.where(first, a, got), jnp.where(first, got, a)]).astype(F32)
+        )
+    return wholes
+
+
+def local_paired(
+    tokens,
+    counts,
+    ln1_gain,
+    ln1_shift,
+    w_qkv,
+    bias_q,
+    bias_v,
+    w_out,
+    bias_out,
+    ln2_gain,
+    ln2_shift,
+    w_fc1,
+    bias_fc1,
+    w_fc2,
+    bias_fc2,
+    cotangent,
+):
+    place = Place()
+    odd = place.z % 2
+    short = jnp.argmin(counts).astype(jnp.int32)
+    full_one = jnp.where(short == 0, 1, 0)
+    full_two = jnp.where(short == 2, 1, 2)
+    slots = (jnp.where(odd == 0, full_one, full_two), jnp.where(odd == 0, full_two, full_one), short)
+    tables = (FIRST_TO, SECOND_TO, FIRST_TO)
+
+    def bring(array):
+        return [
+            lax.ppermute(
+                lax.dynamic_index_in_dim(array, slot, 0, keepdims=False),
+                ("dp", "blk"),
+                column_pairs(table),
+            )
+            for slot, table in zip(slots, tables)
+        ]
+
+    def give_back(pieces):
+        home = [
+            lax.ppermute(
+                piece, ("dp", "blk"), [(target, source) for source, target in column_pairs(table)]
+            )
+            for piece, table in zip(pieces, tables)
+        ]
+        return jnp.stack(
+            [
+                jnp.where(slots[0] == i, home[0], jnp.where(slots[1] == i, home[1], home[2]))
+                for i in range(3)
+            ]
+        )
+
+    vecs_one = jnp.stack([ln1_gain, ln1_shift, bias_q, bias_v]).astype(F32)
+    vecs_two = jnp.stack([bias_out, ln2_gain, ln2_shift, bias_fc2]).astype(F32)
+    b1 = bias_fc1.reshape(1, -1).astype(F32)
+
+    xs = bring(tokens)
+    cots = bring(cotangent)
+    q_full, kv_full = project(xs[:2], vecs_one, w_qkv)
+    kv_other = swap(kv_full, "dp", 1)
+    q_short, kv_short = project(xs[2:], vecs_one, w_qkv)
+    kv_near = swap(kv_short, "blk", 1)
+    kv_pair = jnp.concatenate(
+        [jnp.where(odd == 0, kv_short, kv_near), jnp.where(odd == 0, kv_near, kv_short)], axis=1
+    )
+    kv_far = swap(kv_pair, "dp", 1)
+    first_core = place.core == 0
+    kv_head = jnp.where(first_core, kv_pair, kv_far)
+    spare = -(-(SHORT - kv_head.shape[1]) // LANES) * LANES
+    kv_tail = jnp.where(first_core, kv_far[:, :spare], kv_pair[:, :spare])
+
+    seq = 2 * kv_full.shape[1]
+    att_full, t_full = attend(q_full, [kv_full, kv_other], seq, 768, 384)
+    att_short, t_short = attend(q_short, [kv_head, kv_tail], SHORT, 384, 384)
+    (o1, o2, o3, back_att, back_mid, gw1, gw2, gw_out, gb1, sums_two) = feed(
+        att_full, att_short, xs, cots, w_out, vecs_two, w_fc1, b1, w_fc2, 512
+    )
+    output = give_back([o1, o2, o3])
+    early = sum_apart([gw1, gw2, gw_out], place)
+
+    n_full = q_full.shape[0]
+    dq_full, own_full, sent_full = attend_back(
+        q_full, back_att[:n_full], att_full, t_full, [kv_full, kv_other], seq, 768
+    )
+    got_full = swap(sent_full, "dp", 1)
+    dq_short, d_head, d_tail = attend_back(
+        q_short, back_att[n_full:], att_short, t_short, [kv_head, kv_tail], SHORT, 448
+    )
+    d_tail = jnp.pad(d_tail, ((0, 0), (0, d_head.shape[1] - spare), (0, 0)))
+    got_pair = swap(jnp.where(first_core, d_tail, d_head), "dp", 1)
+    d_pair = add_low(jnp.where(first_core, d_head, d_tail), got_pair)
+    block = kv_short.shape[1]
+    own_short = lax.dynamic_slice_in_dim(d_pair, odd * block, block, 1)
+    got_short = swap(lax.dynamic_slice_in_dim(d_pair, (1 - odd) * block, block, 1), "blk", 1)
+    back, gw_qkv, sums_one = project_grad(
+        xs, vecs_one, dq_full, dq_short, own_full, got_full, own_short, got_short
+    )
+    late = sum_apart([gw_qkv], place)
+    i1, i2, i3, sums_in = input_grad_of(xs, vecs_one, back, w_qkv, back_mid)
+    input_grad = give_back([i1, i2, i3]).astype(F32)
+    grad_w_fc1, grad_w_fc2, grad_w_out = join(early, place)
+    (grad_w_qkv,) = join(late, place)
+    lines = jnp.concatenate(
+        [sums_two[:4], gb1.reshape(-1, 768), sums_one[:2], sums_in[:2]], axis=0
+    )
+    lines = lax.psum(lines, ("dp", "blk"))
+    wide = w_fc1.shape[1] // 768
+    return (
+        output,
+        input_grad,
+        lines[6 + wide],
+        lines[7 + wide],
+        grad_w_qkv,
+        lines[4 + wide],
+        lines[5 + wide],
+        grad_w_out,
+        lines[0],
+        lines[1],
+        lines[2],
+        grad_w_fc1,
+        lines[4 : 4 + wide].reshape(-1),
+        grad_w_fc2,
+        lines[3],
+    )
+
+
 def solution(mesh):
+    paired = mesh.shape["dp"] == 8 and mesh.shape["blk"] == 4
+    chosen = local_paired if paired else local
     return jax.shard_map(
-        local,
+        chosen,
         mesh=mesh,
         in_specs=(
             P("dp", "blk", None),

time: 1730 us -> 626 us (0.36)
  waiting for transfers between devices: 919 us -> 165 us
  matrix products: 394 us -> 0 us
  Pallas kernels: 0 us -> 174 us
  starting transfers between devices: 1.05 us -> 148 us
  local copies, waits for them, and re-layouts: 168 us -> 38.3 us
  other arithmetic: 156 us -> 46.5 us
  blocking collectives: 65.3 us -> 40.9 us
    reduce_scatter x6 -> x0, waiting for transfers between devices: 478 us -> none  [the longest x1 126 us: local(): lax.psum_scatter(key_grads.astype(jnp.bfloat16), 'blk', scatter_dimension...]
    dot_general x33 -> x0, matrix products: 394 us -> none  [the longest x3 64.8 us: block_grads(): jnp.einsum('cqhd,ckhd->chqk', back_heads, value_part, preferred_element_t...]
    all_gather x6 -> x0, waiting for transfers between devices: 360 us -> none  [the longest x1 120 us: local(): lax.all_gather(value_local, 'blk', axis=1, tiled=True)]
    pallas_call x0 -> x9, Pallas kernels: none -> 174 us  [the longest x1 53.4 us: feed(): pl.pallas_call(functools.partial(feed_kernel, steps=steps, tile=tile), gr...]
    ppermute x0 -> x74, waiting for transfers between devices: none -> 165 us  [the longest x62 151 us: swap(): return lax.ppermute(array, axis, flip_pairs(8 if axis == 'dp' else 4, mask))]
    ppermute x0 -> x74, starting transfers between devices: none -> 148 us  [the longest x62 122 us: swap(): return lax.ppermute(array, axis, flip_pairs(8 if axis == 'dp' else 4, mask))]
    psum x1 -> x0, waiting for transfers between devices: 78.3 us -> none  [total_every(): lax.psum(split[2].astype(jnp.bfloat16), 'dp').astype(jnp.float32)]
    reduce_sum x13 -> x0, other arithmetic: 63.1 us -> none  [the longest x3 42.1 us: forward_block(): row_total = row_total * factor + jnp.sum(weights, axis=-1)]
  transfers between devices with their start and end apart: 13 -> 74, of which waited for: 11 -> 26; matrix products, arithmetic and copies ran while one was open for 9% -> 12% of each run, Pallas kernels for 0% -> 19%
where the time goes in v1:
time: 626 us; the launch traced here: 618 us
  Pallas kernels  174 us (28%)
  waiting for transfers between devices  165 us (26%)
  starting transfers between devices  148 us (24%)
  other arithmetic  46.5 us (7%)
  blocking collectives  40.9 us (7%)
  local copies, waits for them, and re-layouts  38.3 us (6%)
    ppermute x62, waiting for transfers between devices, swap(): return lax.ppermute(array, axis, flip_pairs(8 if axis == 'dp' else 4, mask))  151 us
    ppermute x62, starting transfers between devices, swap(): return lax.ppermute(array, axis, flip_pairs(8 if axis == 'dp' else 4, mask))  122 us
    pallas_call x1, Pallas kernels, feed(): pl.pallas_call(functools.partial(feed_kernel, steps=steps, tile=tile), gr...  53.4 us
    pallas_call x2, Pallas kernels, attend_back(): pl.pallas_call(functools.partial(attend_back_kernel, pieces=len(kvs), val...  53.4 us
    psum x1, blocking collectives, local_paired(): lines = lax.psum(lines, ('dp', 'blk'))  40.9 us
    pallas_call x2, Pallas kernels, attend(): pl.pallas_call(functools.partial(attend_kernel, pieces=len(kvs), valid=va...  35.9 us
    convert_element_type x4, other arithmetic, join(): jnp.concatenate([jnp.where(first, a, got), jnp.where(first, got, a)])  14.5 us
    ppermute x6, starting transfers between devices, bring(): lax.ppermute(lax.dynamic_index_in_dim(array, slot, 0, keepdims=False), ('...  14.1 us
  transfers between devices with their start and end apart: 74, of which 26 were waited for; matrix products, arithmetic and copies ran while one was open for 12% of the time, Pallas kernels for 19%

profile of v1, /device:TPU:0, one launch (start us, length us, event | category | flops | bytes accessed | tf_op | source)
XLA Modules:
  0.0 618.1 jit_solution(5850633494606818246)
XLA Ops:
  8.2 3.1 collective-permute-start.1
  13.4 11.6 %collective-permute-done.1.refs_1_.x2 = bf16[384,768]{1,0:T(8,128)(2,1)S(1)} collective-permute-done((bf16[384,768]{1,0:T(8,128)(2,1)S(1)}, bf16[384,768]{1,0:T(8,128)(2,1)S(1)}, u32[]{:S(2)}, u32[]{:S(2)}) %collective-permute-start.1) | collective-permute-done | bytes 589856 | tf_op jit(solution)/shard_map/ppermute | solution.py:904
  25.0 4.7 project.2
  29.7 27.2 %collective-permute-start.2 = (bf16[2,768,768]{2,1,0:T(8,128)(2,1)}, bf16[2,768,768]{2,1,0:T(8,128)(2,1)}, u32[]{:S(2)}, u32[]{:S(2)}) collective-permute-start(bf16[2,768,768]{2,1,0:T(8,128)(2,1)} %get-tuple-element.49.refs_1_.refs_4_), channel_id=1, source_target_pairs={{0,4},{4,0},{8,12},{12,8},{16,20},{20,16},{24,28},{28,24},{1,5},{5... | collective-permute-start | bytes 7077896 | tf_op jit(solution)/shard_map/ppermute | solution.py:819
  56.8 3.4 collective-permute-done.4
  62.0 2.9 collective-permute-start.5
  65.9 6.0 collective-permute-start.6
  71.9 2.0 collective-permute-start.7
  78.2 24.6 %attend.2 = (f32[768,768]{1,0:T(8,128)}, bf16[768,768]{1,0:T(8,128)(2,1)}) custom-call(bf16[768,768]{1,0:T(8,128)(2,1)} %copy-done.8, bf16[2,768,768]{2,1,0:T(8,128)(2,1)} %get-tuple-element.49.refs_1_.refs_4_, bf16[2,768,768]{2,1,0:T(8,128)(2,1)} %collective-permute-done.2.refs_2_.refs_5_), custom_call_target="tpu_custom_call" | custom-call | flops 14495514624 | bytes 4718592 | tf_op jit(solution)/shard_map/attend/pallas_call | solution.py:513
  106.5 11.3 %attend.3 = (f32[384,768]{1,0:T(8,128)}, bf16[384,768]{1,0:T(8,128)(2,1)}) custom-call(bf16[384,768]{1,0:T(8,128)(2,1)} %copy-done.7, bf16[2,768,768]{2,1,0:T(8,128)(2,1)} %broadcast_select_fusion.4.refs_1_.refs_4_, bf16[2,128,768]{2,1,0:T(8,128)(2,1)} %slice_select_fusion.refs_2_.refs_5_), custom_call_target="tpu_custom_call" | custom-call | flops 4227858432 | bytes 2359296 | tf_op jit(solution)/shard_map/attend/pallas_call | solution.py:513
  117.9 53.4 %feed.1 = (bf16[384,768]{1,0:T(8,128)(2,1)}, bf16[384,768]{1,0:T(8,128)(2,1)}, bf16[384,768]{1,0:T(8,128)(2,1)}, bf16[1152,768]{1,0:T(8,128)(2,1)}, f32[1152,768...) custom-call(f32[768,768]{1,0:T(8,128)} %get-tuple-element.50.att_ful, ...), custom_call_target="tpu_custom_call" | custom-call | flops 36691771392 | bytes 41943040 | tf_op jit(solution)/shard_map/feed/pallas_call | solution.py:682
  177.2 2.3 collective-permute-start.35
  182.7 2.1 collective-permute-done.35
  184.8 2.6 collective-permute-done.34
  192.0 15.9 %attend_back.3 = (bf16[384,768]{1,0:T(8,128)(2,1)}, bf16[2,768,768]{2,1,0:T(8,128)(2,1)}, bf16[2,128,768]{2,1,0:T(8,128)(2,1)}) custom-call(bf16[384,768]{1,0:T(8,128)(2,1)} %copy-done.7, bf16[384,768]{1,0:T(8,128)(2,1)} %slice.51.refs_1_, f32[384,768]{1,0:T(8,128)} %get-tuple-element.53.att_short.refs_2_, bf16[384,768]{1,0:T(8,128)(2,1)} %get-tuple-element.60.refs_3_, ...), custom_call_target="tpu_custom_call" | custom-call | flops 10569646080 | bytes 3538944 | tf_op jit(solution)/shard_map/attend_back/pallas_call | solution.py:582
  207.9 2.5 slice.50.refs_1_
  213.9 2.9 pad_select_fusion
  218.8 2.8 collective-permute-start.41
  222.2 9.0 %collective-permute-done.40 = bf16[24,768]{1,0:T(8,128)(2,1)S(1)} collective-permute-done((bf16[24,768]{1,0:T(8,128)(2,1)S(1)}, bf16[24,768]{1,0:T(8,128)(2,1)S(1)}, u32[]{:S(2)}, u32[]{:S(2)}) %collective-permute-start.40) | collective-permute-done | bytes 36896 | tf_op jit(solution)/shard_map/ppermute | solution.py:819
  239.7 37.6 %attend_back.2 = (bf16[768,768]{1,0:T(8,128)(2,1)}, bf16[2,768,768]{2,1,0:T(8,128)(2,1)}, bf16[2,768,768]{2,1,0:T(8,128)(2,1)}) custom-call(bf16[768,768]{1,0:T(8,128)(2,1)} %copy-done.8, bf16[768,768]{1,0:T(8,128)(2,1)} %slice.50.refs_1_, f32[768,768]{1,0:T(8,128)} %get-tuple-element.50.att_full.refs_2_, bf16[768,768]{1,0:T(8,128)(2,1)} %get-tuple-element.58.refs_3_, ...), custom_call_target="tpu_custom_call" | custom-call | flops 36238786560 | bytes 7077888 | tf_op jit(solution)/shard_map/attend_back/pallas_call | solution.py:582
  279.0 6.1 collective-permute-start.11
  292.9 2.6 collective-permute-done.10
  295.5 10.2 %collective-permute-start.60 = (bf16[1536,768]{1,0:T(8,128)(2,1)}, bf16[1536,768]{1,0:T(8,128)(2,1)S(1)}, u32[]{:S(2)}, u32[]{:S(2)}) collective-permute-start(bf16[1536,768]{1,0:T(8,128)(2,1)} %constant_dynamic-slice_fusion.6), channel_id=1, source_target_pairs={{0,4},{4,0},{8,12},{12,8},{16,20},{20,16},{24,28},{28,24},{1,5},{5... | collective-permute-start | bytes 7077896 | tf_op jit(solution)/shard_map/ppermute | solution.py:819
  311.3 3.0 add_convert_fusion.2
  315.6 2.8 add_convert_fusion.1
  318.6 2.0 collective-permute-start.49
  322.9 12.9 %collective-permute-done.49 = bf16[96,3072]{1,0:T(8,128)(2,1)S(1)} collective-permute-done((bf16[96,3072]{1,0:T(8,128)(2,1)S(1)}, bf16[96,3072]{1,0:T(8,128)(2,1)S(1)}, u32[]{:S(2)}, u32[]{:S(2)}) %collective-permute-start.49) | collective-permute-done | bytes 589856 | tf_op jit(solution)/shard_map/ppermute | solution.py:819
  335.8 2.0 collective-permute-start.63
  337.8 10.6 %collective-permute-done.48 = bf16[96,3072]{1,0:T(8,128)(2,1)S(1)} collective-permute-done((bf16[96,3072]{1,0:T(8,128)(2,1)S(1)}, bf16[96,3072]{1,0:T(8,128)(2,1)S(1)}, u32[]{:S(2)}, u32[]{:S(2)}) %collective-permute-start.48) | collective-permute-done | bytes 589856 | tf_op jit(solution)/shard_map/ppermute | solution.py:819
  348.3 2.0 collective-permute-start.62
  351.3 9.8 %collective-permute-done.63 = bf16[384,768]{1,0:T(8,128)(2,1)S(1)} collective-permute-done((bf16[384,768]{1,0:T(8,128)(2,1)S(1)}, bf16[384,768]{1,0:T(8,128)(2,1)S(1)}, u32[]{:S(2)}, u32[]{:S(2)}) %collective-permute-start.63) | collective-permute-done | bytes 589856 | tf_op jit(solution)/shard_map/ppermute | solution.py:819
  361.1 2.1 collective-permute-start.52
  363.2 9.5 %collective-permute-done.62 = bf16[384,768]{1,0:T(8,128)(2,1)S(1)} collective-permute-done((bf16[384,768]{1,0:T(8,128)(2,1)S(1)}, bf16[384,768]{1,0:T(8,128)(2,1)S(1)}, u32[]{:S(2)}, u32[]{:S(2)}) %collective-permute-start.62) | collective-permute-done | bytes 589856 | tf_op jit(solution)/shard_map/ppermute | solution.py:819
  372.8 2.5 collective-permute-start.51
  378.0 6.2 %collective-permute-done.51 = bf16[24,3072]{1,0:T(8,128)(2,1)S(1)} collective-permute-done((bf16[24,3072]{1,0:T(8,128)(2,1)S(1)}, bf16[24,3072]{1,0:T(8,128)(2,1)S(1)}, u32[]{:S(2)}, u32[]{:S(2)}) %collective-permute-start.51) | collective-permute-done | bytes 147488 | tf_op jit(solution)/shard_map/ppermute | solution.py:819
  384.3 3.3 collective-permute-start.64
  387.7 5.7 collective-permute-start.53
  393.4 2.0 collective-permute-done.65
  395.4 2.7 collective-permute-start.55
  399.6 8.9 %collective-permute-done.54 = bf16[24,3072]{1,0:T(8,128)(2,1)S(1)} collective-permute-done((bf16[24,3072]{1,0:T(8,128)(2,1)S(1)}, bf16[24,3072]{1,0:T(8,128)(2,1)S(1)}, u32[]{:S(2)}, u32[]{:S(2)}) %collective-permute-start.54) | collective-permute-done | bytes 147488 | tf_op jit(solution)/shard_map/ppermute | solution.py:819
  411.9 8.9 %collective-permute-done.68 = bf16[96,768]{1,0:T(8,128)(2,1)S(1)} collective-permute-done((bf16[96,768]{1,0:T(8,128)(2,1)S(1)}, bf16[96,768]{1,0:T(8,128)(2,1)S(1)}, u32[]{:S(2)}, u32[]{:S(2)}) %collective-permute-start.68) | collective-permute-done | bytes 147488 | tf_op jit(solution)/shard_map/ppermute | solution.py:819
  420.9 2.0 collective-permute-start.57
  425.9 13.2 %project_grad.1 = (bf16[1152,2304]{1,0:T(8,128)(2,1)}, bf16[768,2304]{1,0:T(8,128)(2,1)}, f32[8,768]{1,0:T(8,128)}) custom-call(bf16[384,768]{1,0:T(8,128)(2,1)} %copy-done.5, bf16[384,768]{1,0:T(8,128)(2,1)} %copy-done.6, bf16[384,768]{1,0:T(8,128)(2,1)} %copy-done.4, f32[4,768]{1,0:T(4,128)} %copy-done.2, bf16[768,768]{1,0:T(8,128)(2,1)} %get-tuple-element.59.dq_full, ...), custom_call_target="tpu_custom_call" | custom-call | flops 4076863488 | bytes 16777216 | tf_op jit(solution)/shard_map/project_grad/pallas_call | solution.py:750
  439.0 2.8 constant_dynamic-slice_fusion.27
  443.6 11.4 %input_grad.1 = (bf16[384,768]{1,0:T(8,128)(2,1)}, bf16[384,768]{1,0:T(8,128)(2,1)}, bf16[384,768]{1,0:T(8,128)(2,1)}, f32[8,768]{1,0:T(8,128)}) custom-call(bf16[384,768]{1,0:T(8,128)(2,1)} %copy-done.5, bf16[384,768]{1,0:T(8,128)(2,1)} %copy-done.6, bf16[384,768]{1,0:T(8,128)(2,1)} %copy-done.4, f32[4,768]{1,0:T(4,128)} %copy-done.2, ...), custom_call_target="tpu_custom_call" | custom-call | flops 4076863488 | bytes 16777216 | tf_op jit(solution)/shard_map/input_grad/pallas_call | solution.py:783
  457.2 40.9 %psum.7 = f32[12,768]{1,0:T(8,128)} all-reduce(f32[12,768]{1,0:T(8,128)} %pad_maximum_fusion.2), channel_id=1, replica_groups=mesh['dp'=8,'blk'=4] {'dp','blk'}, use_global_device_ids=true, to_apply=%region_1.2 | all-reduce | flops 9216 | bytes 73728 | tf_op jit(solution)/shard_map/psum | solution.py:979
  501.1 3.0 collective-permute-start.58
  510.4 2.4 add_convert_fusion.3
  512.9 3.0 collective-permute-start.21
  516.6 14.4 %collective-permute-done.72 = bf16[384,768]{1,0:T(8,128)(2,1)S(1)} collective-permute-done((bf16[384,768]{1,0:T(8,128)(2,1)S(1)}, bf16[384,768]{1,0:T(8,128)(2,1)S(1)}, u32[]{:S(2)}, u32[]{:S(2)}) %collective-permute-start.72) | collective-permute-done | bytes 589856 | tf_op jit(solution)/shard_map/ppermute | solution.py:819
  531.0 2.2 collective-permute-start.19
  533.5 7.0 %collective-permute-done.21 = bf16[96,2304]{1,0:T(8,128)(2,1)S(1)} collective-permute-done((bf16[96,2304]{1,0:T(8,128)(2,1)S(1)}, bf16[96,2304]{1,0:T(8,128)(2,1)S(1)}, u32[]{:S(2)}, u32[]{:S(2)}) %collective-permute-start.21) | collective-permute-done | bytes 442400 | tf_op jit(solution)/shard_map/ppermute | solution.py:819
  541.4 6.4 %collective-permute-done.20 = bf16[96,2304]{1,0:T(8,128)(2,1)S(1)} collective-permute-done((bf16[96,2304]{1,0:T(8,128)(2,1)S(1)}, bf16[96,2304]{1,0:T(8,128)(2,1)S(1)}, u32[]{:S(2)}, u32[]{:S(2)}) %collective-permute-start.20) | collective-permute-done | bytes 442400 | tf_op jit(solution)/shard_map/ppermute | solution.py:819
  548.8 2.0 collective-permute-start.24
  550.8 8.6 %collective-permute-start.23 = (bf16[24,2304]{1,0:T(8,128)(2,1)S(1)}, bf16[24,2304]{1,0:T(8,128)(2,1)S(1)}, u32[]{:S(2)}, u32[]{:S(2)}) collective-permute-start(bf16[24,2304]{1,0:T(8,128)(2,1)S(1)} %get-tuple-element.139), channel_id=1, source_target_pairs={{0,2},{1,3},{2,0},{3,1},{4,6},{5,7},{6,4},{7,5},{8,10},{9,11},{10,... | collective-permute-start | bytes 331784 | tf_op jit(solution)/shard_map/ppermute | solution.py:819
  559.5 10.6 %collective-permute-done.23 = bf16[24,2304]{1,0:T(8,128)(2,1)S(1)} collective-permute-done((bf16[24,2304]{1,0:T(8,128)(2,1)S(1)}, bf16[24,2304]{1,0:T(8,128)(2,1)S(1)}, u32[]{:S(2)}, u32[]{:S(2)}) %collective-permute-start.23) | collective-permute-done | bytes 110624 | tf_op jit(solution)/shard_map/ppermute | solution.py:819
  570.3 2.1 maximum_convert_fusion.3
  572.4 5.5 collective-permute-start.26
  577.9 7.3 %collective-permute-done.26 = bf16[24,2304]{1,0:T(8,128)(2,1)S(1)} collective-permute-done((bf16[24,2304]{1,0:T(8,128)(2,1)S(1)}, bf16[24,2304]{1,0:T(8,128)(2,1)S(1)}, u32[]{:S(2)}, u32[]{:S(2)}) %collective-permute-start.26) | collective-permute-done | bytes 110624 | tf_op jit(solution)/shard_map/ppermute | solution.py:819
  589.3 9.1 %collective-permute-done.28 = bf16[96,2304]{1,0:T(8,128)(2,1)S(1)} collective-permute-done((bf16[96,2304]{1,0:T(8,128)(2,1)S(1)}, bf16[96,2304]{1,0:T(8,128)(2,1)S(1)}, u32[]{:S(2)}, u32[]{:S(2)}) %collective-permute-start.28) | collective-permute-done | bytes 442400 | tf_op jit(solution)/shard_map/ppermute | solution.py:819
  598.4 4.5 collective-permute-done.29
  604.3 5.0 maximum_convert_fusion
  609.6 4.5 maximum_convert_fusion.1
  614.4 3.5 maximum_convert_fusion.2
  (273 shorter events, 97.8 us)
Async XLA Ops:
  8.2 16.8 %collective-permute-start.1 = (bf16[384,768]{1,0:T(8,128)(2,1)S(1)}, bf16[384,768]{1,0:T(8,128)(2,1)S(1)}, u32[]{:S(2)}, u32[]{:S(2)}) collective-permute-start(bf16[384,768]{1,0:T(8,128)(2,1)S(1)} %get-tuple-element.125), channel_id=1, source_target_pairs={{0,1},{1,0},{2,5},{3,4},{4,3},{5,2},{6,7},{7,6},{8,9},{9,8},{10,13... | collective-permute-start | bytes 1769480 | tf_op jit(solution)/shard_map/ppermute | solution.py:904
  13.3 47.0 %collective-permute-start.4 = (bf16[2,384,768]{2,1,0:T(8,128)(2,1)S(1)}, bf16[2,384,768]{2,1,0:T(8,128)(2,1)S(1)}, u32[]{:S(2)}, u32[]{:S(2)}) collective-permute-start(bf16[2,384,768]{2,1,0:T(8,128)(2,1)S(1)} %get-tuple-element.52), channel_id=1, source_target_pairs={{0,1},{1,0},{2,3},{3,2},{4,5},{5,4},{6,7},{7,6},{8,9},{9,8},{10,11... | collective-permute-start | bytes 3538952 | tf_op jit(solution)/shard_map/ppermute | solution.py:819
  29.7 48.5 %collective-permute-start.2 = (bf16[2,768,768]{2,1,0:T(8,128)(2,1)}, bf16[2,768,768]{2,1,0:T(8,128)(2,1)}, u32[]{:S(2)}, u32[]{:S(2)}) collective-permute-start(bf16[2,768,768]{2,1,0:T(8,128)(2,1)} %get-tuple-element.49.refs_1_.refs_4_), channel_id=1, source_target_pairs={{0,4},{4,0},{8,12},{12,8},{16,20},{20,16},{24,28},{28,24},{1,5},{5... | collective-permute-start | bytes 7077896 | tf_op jit(solution)/shard_map/ppermute | solution.py:819
  62.0 40.8 %collective-permute-start.5 = (bf16[2,768,768]{2,1,0:T(8,128)(2,1)}, bf16[2,768,768]{2,1,0:T(8,128)(2,1)}, u32[]{:S(2)}, u32[]{:S(2)}) collective-permute-start(bf16[2,768,768]{2,1,0:T(8,128)(2,1)} %pad_maximum_fusion), channel_id=1, source_target_pairs={{0,4},{4,0},{8,12},{12,8},{16,20},{20,16},{24,28},{28,24},{1,5},{5... | collective-permute-start | bytes 7077896 | tf_op jit(solution)/shard_map/ppermute | solution.py:819
  65.9 52.0 %collective-permute-start.6 = (bf16[384,768]{1,0:T(8,128)(2,1)}, bf16[384,768]{1,0:T(8,128)(2,1)}, u32[]{:S(2)}, u32[]{:S(2)}) collective-permute-start(bf16[384,768]{1,0:T(8,128)(2,1)} %get-tuple-element.121), channel_id=1, source_target_pairs={{0,0},{1,1},{2,4},{3,5},{4,2},{5,3},{6,6},{7,7},{8,8},{9,9},{10,12... | collective-permute-start | bytes 1769480 | tf_op jit(solution)/shard_map/ppermute | solution.py:904
  71.9 46.0 %collective-permute-start.7 = (bf16[384,768]{1,0:T(8,128)(2,1)S(1)}, bf16[384,768]{1,0:T(8,128)(2,1)}, u32[]{:S(2)}, u32[]{:S(2)}) collective-permute-start(bf16[384,768]{1,0:T(8,128)(2,1)S(1)} %get-tuple-element.122), channel_id=1, source_target_pairs={{0,1},{1,0},{2,5},{3,4},{4,3},{5,2},{6,7},{7,6},{8,9},{9,8},{10,13... | collective-permute-start | bytes 1769480 | tf_op jit(solution)/shard_map/ppermute | solution.py:904
  73.9 44.0 %collective-permute-start.8 = (bf16[384,768]{1,0:T(8,128)(2,1)S(1)}, bf16[384,768]{1,0:T(8,128)(2,1)}, u32[]{:S(2)}, u32[]{:S(2)}) collective-permute-start(bf16[384,768]{1,0:T(8,128)(2,1)S(1)} %get-tuple-element.120), channel_id=1, source_target_pairs={{0,0},{1,1},{2,4},{3,5},{4,2},{5,3},{6,6},{7,7},{8,8},{9,9},{10,12... | collective-permute-start | bytes 1769480 | tf_op jit(solution)/shard_map/ppermute | solution.py:904
  187.5 24.6 %collective-permute-start.38 = (bf16[24,768]{1,0:T(8,128)(2,1)S(1)}, bf16[24,768]{1,0:T(8,128)(2,1)S(1)}, u32[]{:S(2)}, u32[]{:S(2)}) collective-permute-start(bf16[24,768]{1,0:T(8,128)(2,1)S(1)} %get-tuple-element.141), channel_id=1, source_target_pairs={{0,3},{1,2},{2,1},{3,0},{4,7},{5,6},{6,5},{7,4},{8,11},{9,10},{10,... | collective-permute-start | bytes 110600 | tf_op jit(solution)/shard_map/ppermute | solution.py:819
  189.3 22.8 %collective-permute-start.37 = (bf16[24,768]{1,0:T(8,128)(2,1)S(1)}, bf16[24,768]{1,0:T(8,128)(2,1)S(1)}, u32[]{:S(2)}, u32[]{:S(2)}) collective-permute-start(bf16[24,768]{1,0:T(8,128)(2,1)S(1)} %get-tuple-element.142), channel_id=1, source_target_pairs={{0,2},{1,3},{2,0},{3,1},{4,6},{5,7},{6,4},{7,5},{8,10},{9,11},{10,... | collective-permute-start | bytes 110600 | tf_op jit(solution)/shard_map/ppermute | solution.py:819
  190.5 21.7 %collective-permute-start.36 = (bf16[24,768]{1,0:T(8,128)(2,1)S(1)}, bf16[24,768]{1,0:T(8,128)(2,1)S(1)}, u32[]{:S(2)}, u32[]{:S(2)}) collective-permute-start(bf16[24,768]{1,0:T(8,128)(2,1)S(1)} %get-tuple-element.140), channel_id=1, source_target_pairs={{0,1},{1,0},{2,3},{3,2},{4,5},{5,4},{6,7},{7,6},{8,9},{9,8},{10,11... | collective-permute-start | bytes 110600 | tf_op jit(solution)/shard_map/ppermute | solution.py:819
  210.4 77.5 %collective-permute-start.9 = (bf16[384,768]{1,0:T(8,128)(2,1)}, bf16[384,768]{1,0:T(8,128)(2,1)S(1)}, u32[]{:S(2)}, u32[]{:S(2)}) collective-permute-start(bf16[384,768]{1,0:T(8,128)(2,1)} %get-tuple-element.54), channel_id=1, source_target_pairs={{0,0},{1,1},{4,2},{5,3},{2,4},{3,5},{6,6},{7,7},{8,8},{9,9},{12,10... | collective-permute-start | bytes 1769480 | tf_op jit(solution)/shard_map/ppermute | solution.py:914
  216.8 94.5 %collective-permute-start.13 = (bf16[2,768,768]{2,1,0:T(8,128)(2,1)}, bf16[2,768,768]{2,1,0:T(8,128)(2,1)}, u32[]{:S(2)}, u32[]{:S(2)}) collective-permute-start(bf16[2,768,768]{2,1,0:T(8,128)(2,1)} %pad_select_fusion), channel_id=1, source_target_pairs={{0,4},{4,0},{8,12},{12,8},{16,20},{20,16},{24,28},{28,24},{1,5},{5... | collective-permute-start | bytes 7077896 | tf_op jit(solution)/shard_map/ppermute | solution.py:819
  218.6 12.5 %collective-permute-start.40 = (bf16[24,768]{1,0:T(8,128)(2,1)S(1)}, bf16[24,768]{1,0:T(8,128)(2,1)S(1)}, u32[]{:S(2)}, u32[]{:S(2)}) collective-permute-start(bf16[24,768]{1,0:T(8,128)(2,1)S(1)} %get-tuple-element.92), channel_id=1, source_target_pairs={{0,2},{1,3},{2,0},{3,1},{4,6},{5,7},{6,4},{7,5},{8,10},{9,11},{10,... | collective-permute-start | bytes 110600 | tf_op jit(solution)/shard_map/ppermute | solution.py:819
  218.8 13.0 %collective-permute-start.41 = (bf16[24,768]{1,0:T(8,128)(2,1)S(1)}, bf16[24,768]{1,0:T(8,128)(2,1)S(1)}, u32[]{:S(2)}, u32[]{:S(2)}) collective-permute-start(bf16[24,768]{1,0:T(8,128)(2,1)S(1)} %get-tuple-element.92), channel_id=1, source_target_pairs={{0,3},{1,2},{2,1},{3,0},{4,7},{5,6},{6,5},{7,4},{8,11},{9,10},{10,... | collective-permute-start | bytes 110600 | tf_op jit(solution)/shard_map/ppermute | solution.py:819
  235.5 80.0 %collective-permute-start.46 = (bf16[384,3072]{1,0:T(8,128)(2,1)}, bf16[384,3072]{1,0:T(8,128)(2,1)}, u32[]{:S(2)}, u32[]{:S(2)}) collective-permute-start(bf16[384,3072]{1,0:T(8,128)(2,1)} %constant_dynamic-slice_fusion.13), channel_id=1, source_target_pairs={{0,4},{4,0},{8,12},{12,8},{16,20},{20,16},{24,28},{28,24},{1,5},{5... | collective-permute-start | bytes 7077896 | tf_op jit(solution)/shard_map/ppermute | solution.py:819
  235.5 42.7 %collective-permute-start.43 = (bf16[96,768]{1,0:T(8,128)(2,1)}, bf16[96,768]{1,0:T(8,128)(2,1)}, u32[]{:S(2)}, u32[]{:S(2)}) collective-permute-start(bf16[96,768]{1,0:T(8,128)(2,1)} %constant_dynamic-update-slice_fusion.20), channel_id=1, source_target_pairs={{0,16},{4,20},{8,24},{12,28},{16,0},{20,4},{24,8},{28,12},{1,17},{... | collective-permute-start | bytes 442376 | tf_op jit(solution)/shard_map/ppermute | solution.py:819
  238.4 40.6 %collective-permute-start.44 = (bf16[96,768]{1,0:T(8,128)(2,1)}, bf16[96,768]{1,0:T(8,128)(2,1)}, u32[]{:S(2)}, u32[]{:S(2)}) collective-permute-start(bf16[96,768]{1,0:T(8,128)(2,1)} %constant_dynamic-update-slice_fusion.20), channel_id=1, source_target_pairs={{0,24},{4,28},{8,16},{12,20},{16,8},{20,12},{24,0},{28,4},{1,25},{... | collective-permute-start | bytes 442376 | tf_op jit(solution)/shard_map/ppermute | solution.py:819
  278.2 17.3 %collective-permute-start.10 = (bf16[384,768]{1,0:T(8,128)(2,1)}, bf16[384,768]{1,0:T(8,128)(2,1)}, u32[]{:S(2)}, u32[]{:S(2)}) collective-permute-start(bf16[384,768]{1,0:T(8,128)(2,1)} %get-tuple-element.55), channel_id=1, source_target_pairs={{1,0},{0,1},{5,2},{4,3},{3,4},{2,5},{7,6},{6,7},{9,8},{8,9},{13,10... | collective-permute-start | bytes 1769480 | tf_op jit(solution)/shard_map/ppermute | solution.py:914
  279.0 16.5 %collective-permute-start.11 = (bf16[384,768]{1,0:T(8,128)(2,1)}, bf16[384,768]{1,0:T(8,128)(2,1)}, u32[]{:S(2)}, u32[]{:S(2)}) collective-permute-start(bf16[384,768]{1,0:T(8,128)(2,1)} %get-tuple-element.56), channel_id=1, source_target_pairs={{0,0},{1,1},{4,2},{5,3},{2,4},{3,5},{6,6},{7,7},{8,8},{9,9},{12,10... | collective-permute-start | bytes 1769480 | tf_op jit(solution)/shard_map/ppermute | solution.py:914
  288.0 20.6 %collective-permute-start.45 = (bf16[384,768]{1,0:T(8,128)(2,1)S(1)}, bf16[384,768]{1,0:T(8,128)(2,1)}, u32[]{:S(2)}, u32[]{:S(2)}) collective-permute-start(bf16[384,768]{1,0:T(8,128)(2,1)S(1)} %constant_dynamic-update-slice_fusion.16), channel_id=1, source_target_pairs={{0,4},{4,0},{8,12},{12,8},{16,20},{20,16},{24,28},{28,24},{1,5},{5... | collective-permute-start | bytes 1769480 | tf_op jit(solution)/shard_map/ppermute | solution.py:819
  295.5 128.0 %collective-permute-start.12 = (bf16[2,768,768]{2,1,0:T(8,128)(2,1)}, bf16[2,768,768]{2,1,0:T(8,128)(2,1)S(1)}, u32[]{:S(2)}, u32[]{:S(2)}) collective-permute-start(bf16[2,768,768]{2,1,0:T(8,128)(2,1)} %get-tuple-element.63), channel_id=1, source_target_pairs={{0,4},{4,0},{8,12},{12,8},{16,20},{20,16},{24,28},{28,24},{1,5},{5... | collective-permute-start | bytes 7077896 | tf_op jit(solution)/shard_map/ppermute | solution.py:819
  295.5 26.4 %collective-permute-start.60 = (bf16[1536,768]{1,0:T(8,128)(2,1)}, bf16[1536,768]{1,0:T(8,128)(2,1)S(1)}, u32[]{:S(2)}, u32[]{:S(2)}) collective-permute-start(bf16[1536,768]{1,0:T(8,128)(2,1)} %constant_dynamic-slice_fusion.6), channel_id=1, source_target_pairs={{0,4},{4,0},{8,12},{12,8},{16,20},{20,16},{24,28},{28,24},{1,5},{5... | collective-permute-start | bytes 7077896 | tf_op jit(solution)/shard_map/ppermute | solution.py:819
  315.6 109.3 %collective-permute-start.14 = (bf16[2,384,768]{2,1,0:T(8,128)(2,1)S(1)}, bf16[2,384,768]{2,1,0:T(8,128)(2,1)S(1)}, u32[]{:S(2)}, u32[]{:S(2)}) collective-permute-start(bf16[2,384,768]{2,1,0:T(8,128)(2,1)S(1)} %get-tuple-element.107), channel_id=1, source_target_pairs={{0,1},{1,0},{2,3},{3,2},{4,5},{5,4},{6,7},{7,6},{8,9},{9,8},{10,11... | collective-permute-start | bytes 3538952 | tf_op jit(solution)/shard_map/ppermute | solution.py:819
  318.6 17.2 %collective-permute-start.49 = (bf16[96,3072]{1,0:T(8,128)(2,1)S(1)}, bf16[96,3072]{1,0:T(8,128)(2,1)S(1)}, u32[]{:S(2)}, u32[]{:S(2)}) collective-permute-start(bf16[96,3072]{1,0:T(8,128)(2,1)S(1)} %get-tuple-element.105), channel_id=1, source_target_pairs={{0,24},{4,28},{8,16},{12,20},{16,8},{20,12},{24,0},{28,4},{1,25},{... | collective-permute-start | bytes 1769480 | tf_op jit(solution)/shard_map/ppermute | solution.py:819
  320.6 27.7 %collective-permute-start.48 = (bf16[96,3072]{1,0:T(8,128)(2,1)S(1)}, bf16[96,3072]{1,0:T(8,128)(2,1)S(1)}, u32[]{:S(2)}, u32[]{:S(2)}) collective-permute-start(bf16[96,3072]{1,0:T(8,128)(2,1)S(1)} %get-tuple-element.106), channel_id=1, source_target_pairs={{0,16},{4,20},{8,24},{12,28},{16,0},{20,4},{24,8},{28,12},{1,17},{... | collective-permute-start | bytes 1769480 | tf_op jit(solution)/shard_map/ppermute | solution.py:819
  321.9 28.5 %collective-permute-start.47 = (bf16[96,3072]{1,0:T(8,128)(2,1)S(1)}, bf16[96,3072]{1,0:T(8,128)(2,1)S(1)}, u32[]{:S(2)}, u32[]{:S(2)}) collective-permute-start(bf16[96,3072]{1,0:T(8,128)(2,1)S(1)} %get-tuple-element.104), channel_id=1, source_target_pairs={{0,8},{4,12},{8,0},{12,4},{16,24},{20,28},{24,16},{28,20},{1,9},{5... | collective-permute-start | bytes 1769480 | tf_op jit(solution)/shard_map/ppermute | solution.py:819
  335.8 25.3 %collective-permute-start.63 = (bf16[384,768]{1,0:T(8,128)(2,1)S(1)}, bf16[384,768]{1,0:T(8,128)(2,1)S(1)}, u32[]{:S(2)}, u32[]{:S(2)}) collective-permute-start(bf16[384,768]{1,0:T(8,128)(2,1)S(1)} %get-tuple-element.102), channel_id=1, source_target_pairs={{0,24},{4,28},{8,16},{12,20},{16,8},{20,12},{24,0},{28,4},{1,25},{... | collective-permute-start | bytes 1769480 | tf_op jit(solution)/shard_map/ppermute | solution.py:819
  348.3 24.4 %collective-permute-start.62 = (bf16[384,768]{1,0:T(8,128)(2,1)S(1)}, bf16[384,768]{1,0:T(8,128)(2,1)S(1)}, u32[]{:S(2)}, u32[]{:S(2)}) collective-permute-start(bf16[384,768]{1,0:T(8,128)(2,1)S(1)} %get-tuple-element.103), channel_id=1, source_target_pairs={{0,16},{4,20},{8,24},{12,28},{16,0},{20,4},{24,8},{28,12},{1,17},{... | collective-permute-start | bytes 1769480 | tf_op jit(solution)/shard_map/ppermute | solution.py:819
  350.4 24.8 %collective-permute-start.61 = (bf16[384,768]{1,0:T(8,128)(2,1)S(1)}, bf16[384,768]{1,0:T(8,128)(2,1)S(1)}, u32[]{:S(2)}, u32[]{:S(2)}) collective-permute-start(bf16[384,768]{1,0:T(8,128)(2,1)S(1)} %get-tuple-element.101), channel_id=1, source_target_pairs={{0,8},{4,12},{8,0},{12,4},{16,24},{20,28},{24,16},{28,20},{1,9},{5... | collective-permute-start | bytes 1769480 | tf_op jit(solution)/shard_map/ppermute | solution.py:819
  361.1 15.3 %collective-permute-start.52 = (bf16[24,3072]{1,0:T(8,128)(2,1)S(1)}, bf16[24,3072]{1,0:T(8,128)(2,1)S(1)}, u32[]{:S(2)}, u32[]{:S(2)}) collective-permute-start(bf16[24,3072]{1,0:T(8,128)(2,1)S(1)} %get-tuple-element.132), channel_id=1, source_target_pairs={{0,3},{1,2},{2,1},{3,0},{4,7},{5,6},{6,5},{7,4},{8,11},{9,10},{10,... | collective-permute-start | bytes 442376 | tf_op jit(solution)/shard_map/ppermute | solution.py:819
  372.8 11.5 %collective-permute-start.51 = (bf16[24,3072]{1,0:T(8,128)(2,1)S(1)}, bf16[24,3072]{1,0:T(8,128)(2,1)S(1)}, u32[]{:S(2)}, u32[]{:S(2)}) collective-permute-start(bf16[24,3072]{1,0:T(8,128)(2,1)S(1)} %get-tuple-element.133), channel_id=1, source_target_pairs={{0,2},{1,3},{2,0},{3,1},{4,6},{5,7},{6,4},{7,5},{8,10},{9,11},{10,... | collective-permute-start | bytes 442376 | tf_op jit(solution)/shard_map/ppermute | solution.py:819
  375.2 9.1 %collective-permute-start.50 = (bf16[24,3072]{1,0:T(8,128)(2,1)S(1)}, bf16[24,3072]{1,0:T(8,128)(2,1)S(1)}, u32[]{:S(2)}, u32[]{:S(2)}) collective-permute-start(bf16[24,3072]{1,0:T(8,128)(2,1)S(1)} %get-tuple-element.131), channel_id=1, source_target_pairs={{0,1},{1,0},{2,3},{3,2},{4,5},{5,4},{6,7},{7,6},{8,9},{9,8},{10,11... | collective-permute-start | bytes 442376 | tf_op jit(solution)/shard_map/ppermute | solution.py:819
  376.4 11.3 %collective-permute-start.66 = (bf16[96,768]{1,0:T(8,128)(2,1)S(1)}, bf16[96,768]{1,0:T(8,128)(2,1)S(1)}, u32[]{:S(2)}, u32[]{:S(2)}) collective-permute-start(bf16[96,768]{1,0:T(8,128)(2,1)S(1)} %get-tuple-element.129), channel_id=1, source_target_pairs={{0,3},{1,2},{2,1},{3,0},{4,7},{5,6},{6,5},{7,4},{8,11},{9,10},{10,... | collective-permute-start | bytes 442376 | tf_op jit(solution)/shard_map/ppermute | solution.py:819
  384.3 11.1 %collective-permute-start.65 = (bf16[96,768]{1,0:T(8,128)(2,1)S(1)}, bf16[96,768]{1,0:T(8,128)(2,1)S(1)}, u32[]{:S(2)}, u32[]{:S(2)}) collective-permute-start(bf16[96,768]{1,0:T(8,128)(2,1)S(1)} %get-tuple-element.130), channel_id=1, source_target_pairs={{0,2},{1,3},{2,0},{3,1},{4,6},{5,7},{6,4},{7,5},{8,10},{9,11},{10,... | collective-permute-start | bytes 442376 | tf_op jit(solution)/shard_map/ppermute | solution.py:819
  384.3 11.1 %collective-permute-start.64 = (bf16[96,768]{1,0:T(8,128)(2,1)S(1)}, bf16[96,768]{1,0:T(8,128)(2,1)S(1)}, u32[]{:S(2)}, u32[]{:S(2)}) collective-permute-start(bf16[96,768]{1,0:T(8,128)(2,1)S(1)} %get-tuple-element.128), channel_id=1, source_target_pairs={{0,1},{1,0},{2,3},{3,2},{4,5},{5,4},{6,7},{7,6},{8,9},{9,8},{10,11... | collective-permute-start | bytes 442376 | tf_op jit(solution)/shard_map/ppermute | solution.py:819
  387.7 11.0 %collective-permute-start.53 = (bf16[24,3072]{1,0:T(8,128)(2,1)S(1)}, bf16[24,3072]{1,0:T(8,128)(2,1)S(1)}, u32[]{:S(2)}, u32[]{:S(2)}) collective-permute-start(bf16[24,3072]{1,0:T(8,128)(2,1)S(1)} %get-tuple-element.90), channel_id=1, source_target_pairs={{0,1},{1,0},{2,3},{3,2},{4,5},{5,4},{6,7},{7,6},{8,9},{9,8},{10,11... | collective-permute-start | bytes 442376 | tf_op jit(solution)/shard_map/ppermute | solution.py:819
  395.3 13.2 %collective-permute-start.54 = (bf16[24,3072]{1,0:T(8,128)(2,1)S(1)}, bf16[24,3072]{1,0:T(8,128)(2,1)S(1)}, u32[]{:S(2)}, u32[]{:S(2)}) collective-permute-start(bf16[24,3072]{1,0:T(8,128)(2,1)S(1)} %get-tuple-element.90), channel_id=1, source_target_pairs={{0,2},{1,3},{2,0},{3,1},{4,6},{5,7},{6,4},{7,5},{8,10},{9,11},{10,... | collective-permute-start | bytes 442376 | tf_op jit(solution)/shard_map/ppermute | solution.py:819
  395.4 13.2 %collective-permute-start.55 = (bf16[24,3072]{1,0:T(8,128)(2,1)S(1)}, bf16[24,3072]{1,0:T(8,128)(2,1)S(1)}, u32[]{:S(2)}, u32[]{:S(2)}) collective-permute-start(bf16[24,3072]{1,0:T(8,128)(2,1)S(1)} %get-tuple-element.90), channel_id=1, source_target_pairs={{0,3},{1,2},{2,1},{3,0},{4,7},{5,6},{6,5},{7,4},{8,11},{9,10},{10,... | collective-permute-start | bytes 442376 | tf_op jit(solution)/shard_map/ppermute | solution.py:819
  398.7 11.4 %collective-permute-start.67 = (bf16[96,768]{1,0:T(8,128)(2,1)S(1)}, bf16[96,768]{1,0:T(8,128)(2,1)S(1)}, u32[]{:S(2)}, u32[]{:S(2)}) collective-permute-start(bf16[96,768]{1,0:T(8,128)(2,1)S(1)} %get-tuple-element.88), channel_id=1, source_target_pairs={{0,1},{1,0},{2,3},{3,2},{4,5},{5,4},{6,7},{7,6},{8,9},{9,8},{10,11... | collective-permute-start | bytes 442376 | tf_op jit(solution)/shard_map/ppermute | solution.py:819
  408.6 12.3 %collective-permute-start.68 = (bf16[96,768]{1,0:T(8,128)(2,1)S(1)}, bf16[96,768]{1,0:T(8,128)(2,1)S(1)}, u32[]{:S(2)}, u32[]{:S(2)}) collective-permute-start(bf16[96,768]{1,0:T(8,128)(2,1)S(1)} %get-tuple-element.88), channel_id=1, source_target_pairs={{0,2},{1,3},{2,0},{3,1},{4,6},{5,7},{6,4},{7,5},{8,10},{9,11},{10,... | collective-permute-start | bytes 442376 | tf_op jit(solution)/shard_map/ppermute | solution.py:819
  408.6 14.3 %collective-permute-start.69 = (bf16[96,768]{1,0:T(8,128)(2,1)S(1)}, bf16[96,768]{1,0:T(8,128)(2,1)S(1)}, u32[]{:S(2)}, u32[]{:S(2)}) collective-permute-start(bf16[96,768]{1,0:T(8,128)(2,1)S(1)} %get-tuple-element.88), channel_id=1, source_target_pairs={{0,3},{1,2},{2,1},{3,0},{4,7},{5,6},{6,5},{7,4},{8,11},{9,10},{10,... | collective-permute-start | bytes 442376 | tf_op jit(solution)/shard_map/ppermute | solution.py:819
  410.1 96.2 %collective-permute-start.56 = (bf16[96,3072]{1,0:T(8,128)(2,1)S(1)}, bf16[96,3072]{1,0:T(8,128)(2,1)}, u32[]{:S(2)}, u32[]{:S(2)}) collective-permute-start(bf16[96,3072]{1,0:T(8,128)(2,1)S(1)} %constant_dynamic-update-slice_fusion.12), channel_id=1, source_target_pairs={{0,8},{4,12},{8,0},{12,4},{16,24},{20,28},{24,16},{28,20},{1,9},{5... | collective-permute-start | bytes 1769480 | tf_op jit(solution)/shard_map/ppermute | solution.py:819
  420.9 88.4 %collective-permute-start.57 = (bf16[96,3072]{1,0:T(8,128)(2,1)S(1)}, bf16[96,3072]{1,0:T(8,128)(2,1)}, u32[]{:S(2)}, u32[]{:S(2)}) collective-permute-start(bf16[96,3072]{1,0:T(8,128)(2,1)S(1)} %constant_dynamic-update-slice_fusion.12), channel_id=1, source_target_pairs={{0,16},{4,20},{8,24},{12,28},{16,0},{20,4},{24,8},{28,12},{1,17},{... | collective-permute-start | bytes 1769480 | tf_op jit(solution)/shard_map/ppermute | solution.py:819
  423.0 78.1 %collective-permute-start.70 = (bf16[384,768]{1,0:T(8,128)(2,1)S(1)}, bf16[384,768]{1,0:T(8,128)(2,1)}, u32[]{:S(2)}, u32[]{:S(2)}) collective-permute-start(bf16[384,768]{1,0:T(8,128)(2,1)S(1)} %constant_dynamic-update-slice_fusion.4), channel_id=1, source_target_pairs={{0,8},{4,12},{8,0},{12,4},{16,24},{20,28},{24,16},{28,20},{1,9},{5... | collective-permute-start | bytes 1769480 | tf_op jit(solution)/shard_map/ppermute | solution.py:819
  423.6 81.6 %collective-permute-start.71 = (bf16[384,768]{1,0:T(8,128)(2,1)S(1)}, bf16[384,768]{1,0:T(8,128)(2,1)}, u32[]{:S(2)}, u32[]{:S(2)}) collective-permute-start(bf16[384,768]{1,0:T(8,128)(2,1)S(1)} %constant_dynamic-update-slice_fusion.4), channel_id=1, source_target_pairs={{0,16},{4,20},{8,24},{12,28},{16,0},{20,4},{24,8},{28,12},{1,17},{... | collective-permute-start | bytes 1769480 | tf_op jit(solution)/shard_map/ppermute | solution.py:819
  441.9 68.5 %collective-permute-start.18 = (bf16[384,2304]{1,0:T(8,128)(2,1)}, bf16[384,2304]{1,0:T(8,128)(2,1)}, u32[]{:S(2)}, u32[]{:S(2)}) collective-permute-start(bf16[384,2304]{1,0:T(8,128)(2,1)} %constant_dynamic-slice_fusion.27), channel_id=1, source_target_pairs={{0,4},{4,0},{8,12},{12,8},{16,20},{20,16},{24,28},{28,24},{1,5},{5... | collective-permute-start | bytes 5308424 | tf_op jit(solution)/shard_map/ppermute | solution.py:819
  501.1 32.2 %collective-permute-start.58 = (bf16[96,3072]{1,0:T(8,128)(2,1)S(1)}, bf16[96,3072]{1,0:T(8,128)(2,1)S(1)}, u32[]{:S(2)}, u32[]{:S(2)}) collective-permute-start(bf16[96,3072]{1,0:T(8,128)(2,1)S(1)} %constant_dynamic-update-slice_fusion.12), channel_id=1, source_target_pairs={{0,24},{4,28},{8,16},{12,20},{16,8},{20,12},{24,0},{28,4},{1,25},{... | collective-permute-start | bytes 1769480 | tf_op jit(solution)/shard_map/ppermute | solution.py:819
  505.2 25.9 %collective-permute-start.72 = (bf16[384,768]{1,0:T(8,128)(2,1)S(1)}, bf16[384,768]{1,0:T(8,128)(2,1)S(1)}, u32[]{:S(2)}, u32[]{:S(2)}) collective-permute-start(bf16[384,768]{1,0:T(8,128)(2,1)S(1)} %constant_dynamic-update-slice_fusion.4), channel_id=1, source_target_pairs={{0,24},{4,28},{8,16},{12,20},{16,8},{20,12},{24,0},{28,4},{1,25},{... | collective-permute-start | bytes 1769480 | tf_op jit(solution)/shard_map/ppermute | solution.py:819
  506.4 42.4 %collective-permute-start.15 = (bf16[384,768]{1,0:T(8,128)(2,1)}, bf16[384,768]{1,0:T(8,128)(2,1)S(1)}, u32[]{:S(2)}, u32[]{:S(2)}) collective-permute-start(bf16[384,768]{1,0:T(8,128)(2,1)} %get-tuple-element.68), channel_id=1, source_target_pairs={{0,0},{1,1},{4,2},{5,3},{2,4},{3,5},{6,6},{7,7},{8,8},{9,9},{12,10... | collective-permute-start | bytes 1769480 | tf_op jit(solution)/shard_map/ppermute | solution.py:914
  512.9 27.6 %collective-permute-start.21 = (bf16[96,2304]{1,0:T(8,128)(2,1)S(1)}, bf16[96,2304]{1,0:T(8,128)(2,1)S(1)}, u32[]{:S(2)}, u32[]{:S(2)}) collective-permute-start(bf16[96,2304]{1,0:T(8,128)(2,1)S(1)} %get-tuple-element.112), channel_id=1, source_target_pairs={{0,24},{4,28},{8,16},{12,20},{16,8},{20,12},{24,0},{28,4},{1,25},{... | collective-permute-start | bytes 1327112 | tf_op jit(solution)/shard_map/ppermute | solution.py:819
  515.9 32.0 %collective-permute-start.20 = (bf16[96,2304]{1,0:T(8,128)(2,1)S(1)}, bf16[96,2304]{1,0:T(8,128)(2,1)S(1)}, u32[]{:S(2)}, u32[]{:S(2)}) collective-permute-start(bf16[96,2304]{1,0:T(8,128)(2,1)S(1)} %get-tuple-element.113), channel_id=1, source_target_pairs={{0,16},{4,20},{8,24},{12,28},{16,0},{20,4},{24,8},{28,12},{1,17},{... | collective-permute-start | bytes 1327112 | tf_op jit(solution)/shard_map/ppermute | solution.py:819
  531.0 17.4 %collective-permute-start.19 = (bf16[96,2304]{1,0:T(8,128)(2,1)S(1)}, bf16[96,2304]{1,0:T(8,128)(2,1)S(1)}, u32[]{:S(2)}, u32[]{:S(2)}) collective-permute-start(bf16[96,2304]{1,0:T(8,128)(2,1)S(1)} %get-tuple-element.111), channel_id=1, source_target_pairs={{0,8},{4,12},{8,0},{12,4},{16,24},{20,28},{24,16},{28,20},{1,9},{5... | collective-permute-start | bytes 1327112 | tf_op jit(solution)/shard_map/ppermute | solution.py:819
  533.3 17.5 %collective-permute-start.16 = (bf16[384,768]{1,0:T(8,128)(2,1)S(1)}, bf16[384,768]{1,0:T(8,128)(2,1)S(1)}, u32[]{:S(2)}, u32[]{:S(2)}) collective-permute-start(bf16[384,768]{1,0:T(8,128)(2,1)S(1)} %copy-done.26), channel_id=1, source_target_pairs={{1,0},{0,1},{5,2},{4,3},{3,4},{2,5},{7,6},{6,7},{9,8},{8,9},{13,10... | collective-permute-start | bytes 1769480 | tf_op jit(solution)/shard_map/ppermute | solution.py:914
  540.5 18.9 %collective-permute-start.17 = (bf16[384,768]{1,0:T(8,128)(2,1)S(1)}, bf16[384,768]{1,0:T(8,128)(2,1)S(1)}, u32[]{:S(2)}, u32[]{:S(2)}) collective-permute-start(bf16[384,768]{1,0:T(8,128)(2,1)S(1)} %copy-done.25), channel_id=1, source_target_pairs={{0,0},{1,1},{4,2},{5,3},{2,4},{3,5},{6,6},{7,7},{8,8},{9,9},{12,10... | collective-permute-start | bytes 1769480 | tf_op jit(solution)/shard_map/ppermute | solution.py:914
  547.8 41.1 %collective-permute-start.59 = (bf16[384,3072]{1,0:T(8,128)(2,1)S(1)}, bf16[384,3072]{1,0:T(8,128)(2,1)S(1)}, u32[]{:S(2)}, u32[]{:S(2)}) collective-permute-start(bf16[384,3072]{1,0:T(8,128)(2,1)S(1)} %constant_dynamic-update-slice_fusion.8), channel_id=1, source_target_pairs={{0,4},{4,0},{8,12},{12,8},{16,20},{20,16},{24,28},{28,24},{1,5},{5... | collective-permute-start | bytes 7077896 | tf_op jit(solution)/shard_map/ppermute | solution.py:819
  548.5 60.8 %collective-permute-start.73 = (bf16[1536,768]{1,0:T(8,128)(2,1)S(1)}, bf16[1536,768]{1,0:T(8,128)(2,1)S(1)}, u32[]{:S(2)}, u32[]{:S(2)}) collective-permute-start(bf16[1536,768]{1,0:T(8,128)(2,1)S(1)} %constant_dynamic-update-slice_fusion), channel_id=1, source_target_pairs={{0,4},{4,0},{8,12},{12,8},{16,20},{20,16},{24,28},{28,24},{1,5},{5... | collective-permute-start | bytes 7077896 | tf_op jit(solution)/shard_map/ppermute | solution.py:819
  548.8 10.7 %collective-permute-start.24 = (bf16[24,2304]{1,0:T(8,128)(2,1)S(1)}, bf16[24,2304]{1,0:T(8,128)(2,1)S(1)}, u32[]{:S(2)}, u32[]{:S(2)}) collective-permute-start(bf16[24,2304]{1,0:T(8,128)(2,1)S(1)} %get-tuple-element.138), channel_id=1, source_target_pairs={{0,3},{1,2},{2,1},{3,0},{4,7},{5,6},{6,5},{7,4},{8,11},{9,10},{10,... | collective-permute-start | bytes 331784 | tf_op jit(solution)/shard_map/ppermute | solution.py:819
  550.8 19.3 %collective-permute-start.23 = (bf16[24,2304]{1,0:T(8,128)(2,1)S(1)}, bf16[24,2304]{1,0:T(8,128)(2,1)S(1)}, u32[]{:S(2)}, u32[]{:S(2)}) collective-permute-start(bf16[24,2304]{1,0:T(8,128)(2,1)S(1)} %get-tuple-element.139), channel_id=1, source_target_pairs={{0,2},{1,3},{2,0},{3,1},{4,6},{5,7},{6,4},{7,5},{8,10},{9,11},{10,... | collective-permute-start | bytes 331784 | tf_op jit(solution)/shard_map/ppermute | solution.py:819
  559.4 10.7 %collective-permute-start.22 = (bf16[24,2304]{1,0:T(8,128)(2,1)S(1)}, bf16[24,2304]{1,0:T(8,128)(2,1)S(1)}, u32[]{:S(2)}, u32[]{:S(2)}) collective-permute-start(bf16[24,2304]{1,0:T(8,128)(2,1)S(1)} %get-tuple-element.137), channel_id=1, source_target_pairs={{0,1},{1,0},{2,3},{3,2},{4,5},{5,4},{6,7},{7,6},{8,9},{9,8},{10,11... | collective-permute-start | bytes 331784 | tf_op jit(solution)/shard_map/ppermute | solution.py:819
  572.4 12.8 %collective-permute-start.26 = (bf16[24,2304]{1,0:T(8,128)(2,1)S(1)}, bf16[24,2304]{1,0:T(8,128)(2,1)S(1)}, u32[]{:S(2)}, u32[]{:S(2)}) collective-permute-start(bf16[24,2304]{1,0:T(8,128)(2,1)S(1)} %get-tuple-element.94), channel_id=1, source_target_pairs={{0,2},{1,3},{2,0},{3,1},{4,6},{5,7},{6,4},{7,5},{8,10},{9,11},{10,... | collective-permute-start | bytes 331784 | tf_op jit(solution)/shard_map/ppermute | solution.py:819
  585.2 13.2 %collective-permute-start.28 = (bf16[96,2304]{1,0:T(8,128)(2,1)S(1)}, bf16[96,2304]{1,0:T(8,128)(2,1)S(1)}, u32[]{:S(2)}, u32[]{:S(2)}) collective-permute-start(bf16[96,2304]{1,0:T(8,128)(2,1)S(1)} %constant_dynamic-update-slice_fusion.28), channel_id=1, source_target_pairs={{0,8},{4,12},{8,0},{12,4},{16,24},{20,28},{24,16},{28,20},{1,9},{5... | collective-permute-start | bytes 1327112 | tf_op jit(solution)/shard_map/ppermute | solution.py:819
  586.0 17.0 %collective-permute-start.29 = (bf16[96,2304]{1,0:T(8,128)(2,1)S(1)}, bf16[96,2304]{1,0:T(8,128)(2,1)S(1)}, u32[]{:S(2)}, u32[]{:S(2)}) collective-permute-start(bf16[96,2304]{1,0:T(8,128)(2,1)S(1)} %constant_dynamic-update-slice_fusion.28), channel_id=1, source_target_pairs={{0,16},{4,20},{8,24},{12,28},{16,0},{20,4},{24,8},{28,12},{1,17},{... | collective-permute-start | bytes 1327112 | tf_op jit(solution)/shard_map/ppermute | solution.py:819
  587.8 16.4 %collective-permute-start.30 = (bf16[96,2304]{1,0:T(8,128)(2,1)S(1)}, bf16[96,2304]{1,0:T(8,128)(2,1)S(1)}, u32[]{:S(2)}, u32[]{:S(2)}) collective-permute-start(bf16[96,2304]{1,0:T(8,128)(2,1)S(1)} %constant_dynamic-update-slice_fusion.28), channel_id=1, source_target_pairs={{0,24},{4,28},{8,16},{12,20},{16,8},{20,12},{24,0},{28,4},{1,25},{... | collective-permute-start | bytes 1327112 | tf_op jit(solution)/shard_map/ppermute | solution.py:819
  604.2 9.9 %collective-permute-start.31 = (bf16[384,2304]{1,0:T(8,128)(2,1)S(1)}, bf16[384,2304]{1,0:T(8,128)(2,1)S(1)}, u32[]{:S(2)}, u32[]{:S(2)}) collective-permute-start(bf16[384,2304]{1,0:T(8,128)(2,1)S(1)} %constant_dynamic-update-slice_fusion.24), channel_id=1, source_target_pairs={{0,4},{4,0},{8,12},{12,8},{16,20},{20,16},{24,28},{28,24},{1,5},{5... | collective-permute-start | bytes 5308424 | tf_op jit(solution)/shard_map/ppermute | solution.py:819
  (45 other events, 538.5 us)
